TPU v7x, 128 devices: a whole 4x4x4 slice. The times are simulated.
128 devices in a mesh: section: 32 (over z, y_lo, x), tensor: 4 (over y_hi, core).
Axes of the slice: x: 4, y: 4 (y_hi: 2, y_lo: 2; y = y_hi * 2 + y_lo), z: 4, core: 2. Of those that a mesh axis runs over, the one named last changes fastest.
Arguments:
- hidden: bfloat16 [512, 12288], P('section', 'tensor'), may hold values from -8 to 8, as said below
- embedding: bfloat16 [51200, 12288], P('section', 'tensor'), may hold values from -1 to 1, as said below
- bottom_grad: bfloat16 [512, 12288], P('section', 'tensor'), may hold values from -6 to 6
- targets: int32 [512], P('section'), may hold values from 0 to 51199
- token_ids: int32 [512], P('section'), may hold values from 0 to 51199
Outputs:
- input_grad: bfloat16 [512, 12288], P('section', 'tensor')
- table_grad: bfloat16 [51200, 12288], P('section', 'tensor')
Inputs may be any that keep to these rules, and one draw needn't show every extreme that they name: `hidden`: activations of order one. `embedding`: entries of order 3 / sqrt(12288).
All inputs are finite; a program needn't handle non-finite values.
Results may differ from a plain program's by a relative error of at most 0.0026.
Values may be sent and summed in bfloat16 or wider, within the bound.
No kernel may reach another device: no remote copies, remote signals or barrier semaphores. Data moves between devices by JAX's collectives and lax.ppermute only.
A program may use at most 128 MiB of HBM per device.

v0:
```python
import jax
import jax.numpy as jnp
from jax import lax
from jax.sharding import PartitionSpec as P


def softmax_probs(logits):
    local_max = jnp.max(logits, axis=1)
    maximum = lax.pmax(local_max, "section")
    denominator = lax.psum(jnp.sum(jnp.exp(logits - maximum[:, None]), axis=1), "section")
    return (jnp.exp(logits - maximum[:, None]) / denominator[:, None]).astype(jnp.bfloat16)


def body(hidden, embedding, bottom_grad, targets, token_ids):
    hidden_all, bottom_all = (
        lax.all_gather(hidden, "section", axis=0, tiled=True),
        lax.all_gather(bottom_grad, "section", axis=0, tiled=True),
    )
    target_all, ids_all = (
        lax.all_gather(targets, "section", axis=0, tiled=True),
        lax.all_gather(token_ids, "section", axis=0, tiled=True),
    )
    vocab_rows = embedding.shape[0]
    vocab_first = lax.axis_index("section") * vocab_rows
    partial_value = lax.dot_general(
        hidden_all, embedding, (((1,), (1,)), ((), ())), preferred_element_type=jnp.float32
    )
    logits = lax.psum(partial_value, "tensor")
    probs = softmax_probs(logits)
    wanted = target_all - vocab_first
    inside = ((wanted >= 0) & (wanted < vocab_rows)).astype(jnp.float32)
    picked = jnp.take(embedding, jnp.clip(wanted, 0, vocab_rows - 1), axis=0).astype(jnp.float32)
    input_grad = lax.psum_scatter(
        jnp.dot(probs, embedding, preferred_element_type=jnp.float32) - picked * inside[:, None],
        "section",
        scatter_dimension=0,
        tiled=True,
    ).astype(jnp.bfloat16)
    columns = jnp.arange(vocab_rows, dtype=jnp.int32)
    all_ids = jnp.concatenate([ids_all, target_all], axis=0)
    id_hits = (all_ids[:, None] - vocab_first == columns[None, :]).astype(jnp.bfloat16)
    lookup_rows = jnp.concatenate([bottom_all, -hidden_all], axis=0)
    head_term = lax.dot_general(
        probs, hidden_all, (((0,), (0,)), ((), ())), preferred_element_type=jnp.float32
    )
    lookup_term = lax.dot_general(
        id_hits, lookup_rows, (((0,), (0,)), ((), ())), preferred_element_type=jnp.float32
    )
    table_grad = (head_term + lookup_term).astype(jnp.bfloat16)
    return (input_grad, table_grad)


def solution(mesh):
    in_specs = (
        P("section", "tensor"),
        P("section", "tensor"),
        P("section", "tensor"),
        P("section"),
        P("section"),
    )
    out_specs = (P("section", "tensor"), P("section", "tensor"))
    return jax.shard_map(body, mesh=mesh, in_specs=in_specs, out_specs=out_specs, check_vma=False)
```

profile of v0, /device:TPU:0, one launch (start us, length us, event | category | flops | bytes accessed | tf_op | source)
XLA Modules:
  0.0 609.7 jit_solution(15016916995710586398)
XLA Ops:
  7.2 0.0 all-gather.3.cloned.1.call-start
  7.2 0.7 all-gather.3.cloned.1.call-update
  7.9 0.0 all-reduce.5.cloned.1.call-start
  7.9 159.6 %all-gather.3.cloned.1.call-done = bf16[512,3072]{1,0:T(8,128)(2,1)} async-done(((bf16[16,3072]{1,0:T(8,128)(2,1)}), bf16[512,3072]{1,0:T(8,128)(2,1)}) %all-gather.3.cloned.1.call-update) | async-done | bytes 3145744 | tf_op jit(solution)/shard_map/all_gather | solution.py:16
  167.5 10.0 %fusion.7 = f32[512,1600]{0,1:T(8,128)} fusion(bf16[512,3072]{1,0:T(8,128)(2,1)} %all-gather.3.cloned.1.call-done, bf16[1600,3072]{1,0:T(8,128)(2,1)} %param.6), kind=kOutput, calls=%fused_computation.18 | convolution fusion | flops 5033164800 | bytes 16252928 | tf_op jit(solution)/shard_map/dot_general | solution.py:25
  177.6 0.0 copy-start.4
  177.6 0.0 copy-start.2
  177.6 0.0 copy-start.3
  177.6 0.0 all-reduce.5.cloned.1.call-update
  177.6 0.0 all-gather.5.cloned.1.call-start
  177.7 0.7 all-gather.5.cloned.1.call-update
  178.3 0.0 reduce-scatter.2.cloned.1.call-start
  178.4 0.0 copy-done.4
  178.4 0.6 dynamic-slice
  179.7 0.0 copy-done.2
  179.7 0.2 dynamic-update-slice
  179.9 0.0 copy-done.3
  179.9 0.2 dynamic-update-slice.1
  180.1 18.2 %all-reduce.2 = (s32[512]{0:T(512)S(1)}, s32[512]{0:T(512)S(1)}) all-reduce(s32[512]{0:T(512)S(1)} %dynamic-update-slice, s32[512]{0:T(512)S(1)} %dynamic-update-slice.1), channel_id=1, replica_groups=mesh['section'=32,'tensor'=4] {'section'}, use_global_device_ids=true, to_apply=%add | all-reduce | flops 1024 | bytes 8192
  198.3 12.3 %gather_fusion = bf16[512,3072]{1,0:T(8,128)(2,1)} fusion(bf16[1600,3072]{1,0:T(8,128)(2,1)} %param.6, s32[1024]{0:T(1024)S(1)} %pad_clamp_fusion), kind=kCustom, calls=%fused_computation | custom fusion | bytes 6293504 | tf_op jit(solution)/shard_map/jit(_take)/gather | solution.py:32
  210.6 45.1 %all-reduce.5.cloned.1.call-done = f32[512,1600]{0,1:T(8,128)} async-done(((f32[512,1600]{0,1:T(8,128)}), f32[512,1600]{0,1:T(8,128)}) %all-reduce.5.cloned.1.call-update) | async-done | bytes 3276816 | tf_op jit(solution)/shard_map/psum | solution.py:28
  255.7 0.0 copy-start
  255.7 2.3 reduce_max.9
  258.1 82.0 %pmax.7 = f32[512]{0:T(512)S(1)} all-reduce(f32[512]{0:T(512)S(1)} %reduce_max.9), channel_id=1, replica_groups=mesh['section'=32,'tensor'=4] {'section'}, use_global_device_ids=true, to_apply=%region_2.0 | all-reduce | flops 512 | bytes 4096 | tf_op jit(solution)/shard_map/pmax | solution.py:9
  340.1 0.0 copy-done
  340.1 0.5 fusion.4
  340.6 77.2 %psum.15 = f32[512]{0:T(512)S(1)} all-reduce(f32[512]{0:T(512)S(1)} %fusion.4), channel_id=1, replica_groups=mesh['section'=32,'tensor'=4] {'section'}, use_global_device_ids=true, to_apply=%region_4.0 | all-reduce | flops 512 | bytes 4096 | tf_op jit(solution)/shard_map/psum | solution.py:10
  417.8 12.7 %multiply_subtract_fusion = f32[512,3072]{1,0:T(8,128)} fusion(bf16[1600,3072]{1,0:T(8,128)(2,1)} %param.6, f32[512]{0:T(512)S(1)} %get-tuple-element.6, bf16[512,3072]{1,0:T(8,128)(2,1)} %gather_fusion, pred[512]{0:T(512)(128)(4,1)S(1)} %get-tuple-element.4, f32[512,1600]{0,1:T(8,128)S(1)} %copy-done, f32[512]{0:T(512)S(1)} %psum.15, f32[512]{0:T(512)S(1)} %pmax.7), kind=kOutput, calls=%fused_computation.6 | convolution fusion | flops 5041913856 | bytes 22551040 | tf_op jit(solution)/shard_map/dot_general | solution.py:34
  430.4 0.0 reduce-scatter.2.cloned.1.call-update
  430.5 0.0 copy-start.1
  430.5 4.3 neg.3
  434.8 0.0 copy-done.1
  434.8 9.5 %fusion.6 = f32[1600,3072]{1,0:T(8,128)} fusion(bf16[512,3072]{1,0:T(8,128)(2,1)S(1)} %copy-done.1, f32[512,1600]{0,1:T(8,128)S(1)} %copy-done, f32[512]{0:T(512)S(1)} %psum.15, f32[512]{0:T(512)S(1)} %pmax.7), kind=kOutput, calls=%fused_computation.17 | convolution fusion | flops 5035622400 | bytes 26087424 | tf_op jit(solution)/shard_map/dot_general | solution.py:43
  444.3 0.0 all-gather.5.cloned.1.call-done
  444.3 18.0 %add_convert_fusion = bf16[1600,3072]{1,0:T(8,128)(2,1)} fusion(f32[1600,3072]{1,0:T(8,128)} %fusion.6, bf16[512,3072]{1,0:T(8,128)(2,1)} %neg.3, bf16[512,3072]{1,0:T(8,128)(2,1)} %all-gather.5.cloned.1.call-done, s32[1024]{0:T(1024)S(1)} %add_subtract_fusion), kind=kOutput, calls=%fused_computation.1 | convolution fusion | flops 10090381312 | bytes 35786752 | tf_op jit(solution)/shard_map/dot_general | solution.py:46
  462.4 139.2 %reduce-scatter.2.cloned.1.call-done = f32[16,3072]{1,0:T(8,128)} async-done(((f32[512,3072]{1,0:T(8,128)}), f32[16,3072]{1,0:T(8,128)}) %reduce-scatter.2.cloned.1.call-update) | async-done | bytes 196624 | tf_op jit(solution)/shard_map/reduce_scatter | solution.py:33
  601.6 1.6 convert_element_type.19
  (5 shorter events, 0.0 us)
Async XLA Ops:
  7.2 160.4 %all-gather.3.cloned.1.call-start = ((), (), s32[]{:S(2)}) async-start(), calls=%async_computation.1 | async-start | bytes 3244032 | tf_op jit(solution)/shard_map/all_gather | solution.py:16
  7.9 247.8 %all-reduce.5.cloned.1.call-start = ((), (), s32[]{:S(2)}) async-start(), calls=%async_computation.2 | async-start | bytes 6553600 | tf_op jit(solution)/shard_map/psum | solution.py:28
  177.6 0.8 copy-start.4
  177.6 2.1 copy-start.2
  177.6 2.3 copy-start.3
  177.6 266.7 %all-gather.5.cloned.1.call-start = ((), (), s32[]{:S(2)}) async-start(), calls=%async_computation.4 | async-start | bytes 3244032 | tf_op jit(solution)/shard_map/all_gather | solution.py:17
  178.3 423.2 %reduce-scatter.2.cloned.1.call-start = ((), (), s32[]{:S(2)}) async-start(), calls=%async_computation.3 | async-start | bytes 6488064 | tf_op jit(solution)/shard_map/reduce_scatter | solution.py:33
  255.7 84.3 %copy-start = (f32[512,1600]{0,1:T(8,128)S(1)}, f32[512,1600]{0,1:T(8,128)}, u32[]{:S(2)}) copy-start(f32[512,1600]{0,1:T(8,128)} %all-reduce.5.cloned.1.call-done) | copy-start | bytes 9830404
  430.5 4.4 copy-start.1
Sparse Core Ops, SparseCore 0:
  9.6 157.8 all-gather.2
  177.7 77.9 all-reduce.4
  257.4 155.1 all-gather.4
  430.6 170.9 reduce-scatter.1
where the time goes:
time: 610 us
  waiting for transfers between devices  345 us (57%)
  blocking collectives  177 us (29%)
  matrix products  50.2 us (8%)
  between operations  14.5 us (2%)
  local copies, waits for them, and re-layouts  13.3 us (2%)
  other arithmetic  8.8 us (1%)
    all_gather x1, waiting for transfers between devices, body(): lax.all_gather(hidden, 'section', axis=0, tiled=True)  160 us
    reduce_scatter x1, waiting for transfers between devices, body(): lax.psum_scatter(jnp.dot(probs, embedding, preferred_element_type=jnp.flo...  139 us
    pmax x1, blocking collectives, softmax_probs(): maximum = lax.pmax(local_max, 'section')  82 us
    psum x1, blocking collectives, softmax_probs(): lax.psum(jnp.sum(jnp.exp(logits - maximum[:, None]), axis=1), 'section')  77.2 us
    psum x1, waiting for transfers between devices, body(): logits = lax.psum(partial_value, 'tensor')  45.1 us
    unnamed x1, blocking collectives  18.2 us
    dot_general x1, matrix products, body(): lax.dot_general(id_hits, lookup_rows, (((0,), (0,)), ((), ())), preferred...  18 us
    dot_general x1, matrix products, body(): jnp.dot(probs, embedding, preferred_element_type=jnp.float32)  12.7 us
  transfers between devices with their start and end apart: 4, of which 3 were waited for; matrix products, arithmetic and copies ran while one was open for 10% of the time, Pallas kernels for 0%

commit v1 on v0

v1 whole, which is shorter than its diff:
```python
import jax
import jax.numpy as jnp
from jax import lax
from jax.sharding import PartitionSpec as P

BF16, F16, F32 = jnp.bfloat16, jnp.float16, jnp.float32
BOTH = ("section", "tensor")
SCALE = 16384.0


def linear(z, yl, x, yh, c):
    return (((z * 2 + yl) * 4 + x) * 2 + yh) * 2 + c


def permute(value, move):
    pairs = []
    for z in range(4):
        for yl in range(2):
            for x in range(4):
                for yh in range(2):
                    for c in range(2):
                        pairs.append((linear(z, yl, x, yh, c), linear(*move(z, yl, x, yh, c))))
    return lax.ppermute(value, BOTH, pairs)


def swap_y(value):
    return permute(value, lambda z, yl, x, yh, c: (z, 1 - yl, x, yh, c))


def swap_core(value):
    return permute(value, lambda z, yl, x, yh, c: (z, yl, x, yh, 1 - c))


def swap_half(value):
    return permute(value, lambda z, yl, x, yh, c: (z, yl, x, 1 - yh, c))


def ring_a(value, k):
    return permute(
        value,
        lambda z, yl, x, yh, c: ((z + k) % 4, yl, x, yh, c) if c == 0 else (z, yl, (x + k) % 4, yh, c),
    )


def ring_b(value, k):
    return permute(
        value,
        lambda z, yl, x, yh, c: (z, yl, (x + k) % 4, yh, c) if c == 0 else ((z + k) % 4, yl, x, yh, c),
    )


def put(buffer, block, index, dim):
    return lax.dynamic_update_slice_in_dim(buffer, jnp.expand_dims(block, dim), index, dim)


def pick(buffer, index, dim):
    return lax.dynamic_index_in_dim(buffer, index, dim, keepdims=False)


def place():
    section, tensor = lax.axis_index("section"), lax.axis_index("tensor")
    z, yl, x, c = section // 8, (section // 4) % 2, section % 4, tensor % 2
    first = jnp.where(c == 0, z, x)
    second = jnp.where(c == 0, x, z)
    return (yl + c) % 2, first, second


def gather_rows(own, cut, where):
    slot, first, second = where
    rows, cols = own.shape
    other = swap_y(own)
    pair = jnp.where(slot == 0, jnp.stack([own, other]), jnp.stack([other, own]))
    line = put(jnp.zeros((2, 4, rows, cols), own.dtype), pair, first, 1)
    for k in (1, 3, 2):
        line = put(line, ring_a(pair, k), (first - k) % 4, 1)
    parts = [(line, second)] + [(ring_b(line, k), (second - k) % 4) for k in (1, 3, 2)]
    main = jnp.zeros((2, 4, 4, rows, cut), own.dtype)
    rest = jnp.zeros((2, 4, 4, rows, cols - cut), own.dtype)
    for block, index in parts:
        main = put(main, block[..., :cut], index, 1)
        rest = put(rest, block[..., cut:], index, 1)
    return main, rest


def scatter_sum(value, where):
    slot, first, second = where

    def ring(total, index, shift):
        out = pick(total, index, 1)
        for k in (1, 3, 2):
            out = out + shift(pick(total, (index + k) % 4, 1).astype(F16), k).astype(F32)
        return out

    line = ring(value, second, ring_b)
    pair = ring(line, first, ring_a)
    return pick(pair, slot, 0) + swap_y(pick(pair, 1 - slot, 0).astype(F16)).astype(F32)


def body(hidden, embedding, bottom_grad, targets, token_ids):
    rows, width = hidden.shape
    vocab_rows = embedding.shape[0]
    vocab_first = lax.axis_index("section") * vocab_rows
    where = place()
    digits = jnp.stack([targets // 256, targets % 256, token_ids // 256, token_ids % 256], axis=1)
    digits = jnp.pad(digits.astype(BF16), ((0, 0), (0, 124)))
    hid, codes = gather_rows(jnp.concatenate([hidden, digits], axis=1), width, where)
    tokens = 32 * rows
    codes = codes.reshape(tokens, 128)[:, :4].astype(jnp.int32)
    target_all = codes[:, 0] * 256 + codes[:, 1]
    ids_all = codes[:, 2] * 256 + codes[:, 3]

    bottom_grad, _ = lax.optimization_barrier((bottom_grad, hid[0, 0, 0, 0, :8]))
    bottom_all, _ = gather_rows(bottom_grad, width, where)

    half = tokens // 2
    dims = (((1,), (1,)), ((), ()))
    sent = lax.dot_general(hid[1].reshape(half, width), embedding, dims, preferred_element_type=F32)
    kept = lax.dot_general(hid[0].reshape(half, width), embedding, dims, preferred_element_type=F32)
    got = swap_core(sent).reshape(4, 4, rows, vocab_rows).transpose(1, 0, 2, 3).reshape(half, vocab_rows)
    partial = kept + got
    logits = partial + swap_half(partial.astype(F16)).astype(F32)

    local_max = jnp.max(logits, axis=1)
    local_sum = jnp.sum(jnp.exp(logits - local_max[:, None]), axis=1)
    stats = jnp.stack([local_max, local_sum]).reshape(1, 2, half)
    stats = lax.all_to_all(jnp.broadcast_to(stats, (32, 2, half)), "section", 0, 0, tiled=True)
    maximum = jnp.max(stats[:, 0], axis=0)
    denominator = jnp.sum(stats[:, 1] * jnp.exp(stats[:, 0] - maximum), axis=0)
    probs_kept = (jnp.exp(logits - maximum[:, None]) / denominator[:, None]).astype(BF16)
    probs_got = swap_core(probs_kept).reshape(4, 4, rows, vocab_rows).transpose(1, 0, 2, 3).reshape(half, vocab_rows)
    probs = jnp.concatenate([probs_kept, probs_got], axis=0)

    columns = jnp.arange(vocab_rows, dtype=jnp.int32)
    wanted = target_all - vocab_first
    inside = ((wanted >= 0) & (wanted < vocab_rows)).astype(F32)
    picked = jnp.take(embedding, jnp.clip(wanted, 0, vocab_rows - 1), axis=0).astype(F32)
    value = jnp.dot(probs, embedding, preferred_element_type=F32) - picked * inside[:, None]
    value = (value * SCALE).reshape(2, 4, 4, rows, width)
    input_grad = (scatter_sum(value, where) * (1.0 / SCALE)).astype(BF16)

    all_ids = jnp.concatenate([ids_all, target_all], axis=0)
    id_hits = (all_ids[:, None] - vocab_first == columns[None, :]).astype(BF16)
    hidden_all = hid.reshape(tokens, width)
    lookup_rows = jnp.concatenate([bottom_all.reshape(tokens, width), -hidden_all], axis=0)
    contract = (((0,), (0,)), ((), ()))
    head_term = lax.dot_general(probs, hidden_all, contract, preferred_element_type=F32)
    lookup_term = lax.dot_general(id_hits, lookup_rows, contract, preferred_element_type=F32)
    table_grad = (head_term + lookup_term).astype(BF16)
    return (input_grad, table_grad)


def solution(mesh):
    split = P("section", "tensor")
    in_specs = (split, split, split, P("section"), P("section"))
    return jax.shard_map(body, mesh=mesh, in_specs=in_specs, out_specs=(split, split), check_vma=False)
```

time: 610 us -> 227 us (0.37)
  waiting for transfers between devices: 345 us -> 76.1 us
  blocking collectives: 177 us -> 0 us
  starting transfers between devices: 0.16 us -> 41.3 us
  local copies, waits for them, and re-layouts: 13.3 us -> 46 us
  between operations: 14.5 us -> 0.97 us
    all_gather x2 -> x0, waiting for transfers between devices: 160 us -> none  [the longest x1 160 us: body(): lax.all_gather(hidden, 'section', axis=0, tiled=True)]
    reduce_scatter x1 -> x0, waiting for transfers between devices: 139 us -> none  [body(): lax.psum_scatter(jnp.dot(probs, embedding, preferred_element_type=jnp.flo...]
    pmax x1 -> x0, blocking collectives: 82 us -> none  [softmax_probs(): maximum = lax.pmax(local_max, 'section')]
    psum x1 -> x0, blocking collectives: 77.2 us -> none  [softmax_probs(): lax.psum(jnp.sum(jnp.exp(logits - maximum[:, None]), axis=1), 'section')]
    ppermute x0 -> x24, waiting for transfers between devices: none -> 67.6 us  [permute(): return lax.ppermute(value, BOTH, pairs)]
    psum x1 -> x0, waiting for transfers between devices: 45.1 us -> none  [body(): logits = lax.psum(partial_value, 'tensor')]
    ppermute x0 -> x24, starting transfers between devices: none -> 35.4 us  [permute(): return lax.ppermute(value, BOTH, pairs)]
    unnamed x1 -> x0, blocking collectives: 18.2 us -> none
  transfers between devices with their start and end apart: 4 -> 25, of which waited for: 3 -> 10; matrix products, arithmetic and copies ran while one was open for 10% -> 36% of each run, Pallas kernels for 0% -> 0%
where the time goes in v1:
time: 227 us; the launch traced here: 226 us
  waiting for transfers between devices  76.1 us (34%)
  matrix products  48.4 us (21%)
  local copies, waits for them, and re-layouts  46 us (20%)
  starting transfers between devices  41.3 us (18%)
  other arithmetic  12.9 us (6%)
    ppermute x24, waiting for transfers between devices, permute(): return lax.ppermute(value, BOTH, pairs)  67.6 us
    ppermute x24, starting transfers between devices, permute(): return lax.ppermute(value, BOTH, pairs)  35.4 us
    dot_general x1, matrix products, body(): lax.dot_general(id_hits, lookup_rows, contract, preferred_element_type=F32)  16.1 us
    gather x1, local copies, waits for them, and re-layouts, body(): jnp.take(embedding, jnp.clip(wanted, 0, vocab_rows - 1), axis=0).astype(F32)  12.1 us
    dot_general x1, matrix products, body(): lax.dot_general(probs, hidden_all, contract, preferred_element_type=F32)  11.9 us
    dynamic_update_slice x18, local copies, waits for them, and re-layouts, put(): lax.dynamic_update_slice_in_dim(buffer, jnp.expand_dims(block, dim), inde...  11.1 us
    dot_general x1, matrix products, body(): jnp.dot(probs, embedding, preferred_element_type=F32)  10 us
    all_to_all x1, waiting for transfers between devices, body(): lax.all_to_all(jnp.broadcast_to(stats, (32, 2, half)), 'section', 0, 0, t...  8.44 us
  transfers between devices with their start and end apart: 25, of which 10 were waited for; matrix products, arithmetic and copies ran while one was open for 36% of the time, Pallas kernels for 0%

profile of v1, /device:TPU:0, one launch (start us, length us, event | category | flops | bytes accessed | tf_op | source)
XLA Modules:
  0.0 225.7 jit_solution(430467269111252121)
XLA Ops:
  0.6 1.7 collective-permute-start.17
  4.5 1.0 collective-permute-done.17
  5.5 1.0 maximum_select_fusion.3
  6.5 4.0 %collective-permute-start.20 = (bf16[2,16,3072]{2,1,0:T(8,128)(2,1)S(1)}, bf16[2,16,3072]{2,1,0:T(8,128)(2,1)S(1)}, u32[]{:S(2)}, u32[]{:S(2)}) collective-permute-start(bf16[2,16,3072]{2,1,0:T(8,128)(2,1)S(1)} %maximum_select_fusion.3), channel_id=1, source_target_pairs={{0,64},{1,9},{2,66},{3,11},{4,68},{5,13},{6,70},{7,15},{8,72},{9,1... | collective-permute-start | bytes 589832 | tf_op jit(solution)/shard_map/ppermute | solution.py:23
  11.3 1.3 collective-permute-start.18
  13.6 1.7 fusion.23
  15.3 1.1 collective-permute-start.3
  16.4 2.6 %collective-permute-start.2 = (bf16[2,16,3200]{2,1,0:T(8,128)(2,1)S(1)}, bf16[2,16,3200]{2,1,0:T(8,128)(2,1)S(1)}, u32[]{:S(2)}, u32[]{:S(2)}) collective-permute-start(bf16[2,16,3200]{2,1,0:T(8,128)(2,1)S(1)} %maximum_select_fusion.1), channel_id=1, source_target_pairs={{0,96},{1,13},{2,98},{3,15},{4,100},{5,1},{6,102},{7,3},{8,104},{9... | collective-permute-start | bytes 614408 | tf_op jit(solution)/shard_map/ppermute | solution.py:23
  21.3 3.0 %collective-permute-start.23 = (bf16[2,4,16,3072]{3,2,1,0:T(8,128)(2,1)}, bf16[2,4,16,3072]{3,2,1,0:T(8,128)(2,1)}, u32[]{:S(2)}, u32[]{:S(2)}) collective-permute-start(bf16[2,4,16,3072]{3,2,1,0:T(8,128)(2,1)} %bitcast_dynamic-update-slice_fusion.9), channel_id=1, source_target_pairs={{0,8},{1,65},{2,10},{3,67},{4,12},{5,69},{6,14},{7,71},{8,0},{9,73... | collective-permute-start | bytes 2359304 | tf_op jit(solution)/shard_map/ppermute | solution.py:23
  24.3 1.1 collective-permute-start.22
  25.5 9.2 %collective-permute-done.1 = bf16[2,16,3200]{2,1,0:T(8,128)(2,1)S(1)} collective-permute-done((bf16[2,16,3200]{2,1,0:T(8,128)(2,1)S(1)}, bf16[2,16,3200]{2,1,0:T(8,128)(2,1)S(1)}, u32[]{:S(2)}, u32[]{:S(2)}) %collective-permute-start.1) | collective-permute-done | bytes 204832 | tf_op jit(solution)/shard_map/ppermute | solution.py:23
  34.7 2.0 collective-permute-start.21
  36.8 1.6 collective-permute-start.4
  38.4 2.1 broadcast.99.clone.1
  40.5 2.4 %bitcast_dynamic-update-slice_fusion.2 = bf16[2,4,4,16,3072]{4,3,2,1,0:T(8,128)(2,1)} fusion(bf16[2,4,4,16,3072]{4,3,2,1,0:T(8,128)(2,1)} %broadcast.99.clone.1, s32[]{:T(128)S(6)} %select_n.247, bf16[2,4,16,3072]{3,2,1,0:T(8,128)(2,1)} %bitcast_dynamic-update-slice_fusion.9), kind=kLoop, calls=%fused_computation.32 | loop fusion | bytes 1572868 | tf_op jit(solution)/shard_map/dynamic_update_slice | solution.py:53
  42.9 1.7 collective-permute-start.5
  45.1 11.9 %collective-permute-done.4 = bf16[2,4,16,3200]{3,2,1,0:T(8,128)(2,1)S(1)} collective-permute-done((bf16[2,4,16,3200]{3,2,1,0:T(8,128)(2,1)S(1)}, bf16[2,4,16,3200]{3,2,1,0:T(8,128)(2,1)S(1)}, u32[]{:S(2)}, u32[]{:S(2)}) %collective-permute-start.4) | collective-permute-done | bytes 819232 | tf_op jit(solution)/shard_map/ppermute | solution.py:23
  56.9 2.3 %collective-permute-start.6 = (bf16[2,4,16,3200]{3,2,1,0:T(8,128)(2,1)S(1)}, bf16[2,4,16,3200]{3,2,1,0:T(8,128)(2,1)S(1)}, u32[]{:S(2)}, u32[]{:S(2)}) collective-permute-start(bf16[2,4,16,3200]{3,2,1,0:T(8,128)(2,1)S(1)} %bitcast_dynamic-update-slice_fusion.6), channel_id=1, source_target_pairs={{0,8},{1,65},{2,10},{3,67},{4,12},{5,69},{6,14},{7,71},{8,0},{9,73... | collective-permute-start | bytes 2457608 | tf_op jit(solution)/shard_map/ppermute | solution.py:23
  59.5 11.3 %collective-permute-done.6 = bf16[2,4,16,3200]{3,2,1,0:T(8,128)(2,1)S(1)} collective-permute-done((bf16[2,4,16,3200]{3,2,1,0:T(8,128)(2,1)S(1)}, bf16[2,4,16,3200]{3,2,1,0:T(8,128)(2,1)S(1)}, u32[]{:S(2)}, u32[]{:S(2)}) %collective-permute-start.6) | collective-permute-done | bytes 819232 | tf_op jit(solution)/shard_map/ppermute | solution.py:23
  71.8 1.4 fusion.48
  73.2 2.8 %fusion.49 = f32[256,1600]{0,1:T(8,128)S(1)} fusion(bf16[256,3072]{1,0:T(8,128)(2,1)S(1)} %bitcast.174, bf16[1600,3072]{1,0:T(8,128)(2,1)S(1)} %bitcast.166), kind=kOutput, calls=%fused_computation.121 | convolution fusion | flops 2516582400 | bytes 13041664 | tf_op jit(solution)/shard_map/dot_general | solution.py:117
  78.2 1.7 collective-permute-done.7
  79.9 2.7 %copy.75 = f32[256,1600]{1,0:T(8,128)} copy(f32[256,1600]{0,1:T(8,128)} %collective-permute-done.7) | data formatting | bytes 3276800 | tf_op jit(solution)/shard_map/ppermute | solution.py:23
  82.5 2.8 %copy.76 = f32[4,4,16,1600]{3,2,1,0:T(8,128)} copy(f32[4,4,16,1600]{3,2,0,1:T(8,128)} %bitcast.168) | data formatting | bytes 3276800 | tf_op jit(solution)/shard_map/transpose | solution.py:119
  85.3 2.6 %copy.77 = f32[256,1600]{0,1:T(8,128)} copy(f32[256,1600]{1,0:T(8,128)} %bitcast.169) | data formatting | bytes 3276800 | tf_op jit(solution)/shard_map/reshape | solution.py:119
  88.0 7.7 %fusion.47 = (f16[256,1600]{0,1:T(8,128)(2,1)S(1)}, f32[256,1600]{0,1:T(8,128)S(1)}) fusion(f32[256,1600]{0,1:T(8,128)} %copy.77, bf16[256,3072]{1,0:T(8,128)(2,1)} %bitcast.173, bf16[1600,3072]{1,0:T(8,128)(2,1)} %param.6), kind=kOutput, calls=%fused_computation.119 | convolution fusion | flops 2517401600 | bytes 15499264 | tf_op jit(solution)/shard_map/dot_general | solution.py:118
  95.6 3.3 %collective-permute-start.8 = (f16[256,1600]{0,1:T(8,128)(2,1)S(1)}, f16[256,1600]{0,1:T(8,128)(2,1)S(1)}, u32[]{:S(2)}, u32[]{:S(2)}) collective-permute-start(f16[256,1600]{0,1:T(8,128)(2,1)S(1)} %get-tuple-element.4), channel_id=1, source_target_pairs={{0,2},{1,3},{2,0},{3,1},{4,6},{5,7},{6,4},{7,5},{8,10},{9,11},{10,... | collective-permute-start | bytes 2457608 | tf_op jit(solution)/shard_map/ppermute | solution.py:23
  98.9 2.1 bitcast_dynamic-update-slice_fusion.3
  103.3 14.2 %collective-permute-done.8 = f16[256,1600]{0,1:T(8,128)(2,1)S(1)} collective-permute-done((f16[256,1600]{0,1:T(8,128)(2,1)S(1)}, f16[256,1600]{0,1:T(8,128)(2,1)S(1)}, u32[]{:S(2)}, u32[]{:S(2)}) %collective-permute-start.8) | collective-permute-done | bytes 819232 | tf_op jit(solution)/shard_map/ppermute | solution.py:23
  119.1 5.9 %all-to-all-start = ((f32[32,2,256]{2,1,0:T(2,128)}), f32[32,2,256]{2,1,0:T(2,128)}, u32[]{:S(2)}, u32[]{:S(2)}) async-start(f32[32,2,256]{2,1,0:T(2,128)} %broadcast_in_dim.95), calls=%async_computation | async-start | bytes 131072 | tf_op jit(solution)/shard_map/all_to_all | solution.py:126
  125.0 8.4 %all-to-all-done = f32[32,2,256]{2,1,0:T(2,128)} async-done(((f32[32,2,256]{2,1,0:T(2,128)}), f32[32,2,256]{2,1,0:T(2,128)}, u32[]{:S(2)}, u32[]{:S(2)}) %all-to-all-start) | async-done | bytes 65568 | tf_op jit(solution)/shard_map/all_to_all | solution.py:126
  133.5 1.0 slice_reduce_fusion
  134.5 2.9 %divide_convert_fusion = bf16[256,1600]{0,1:T(8,128)(2,1)} fusion(f32[256]{0:T(256)S(1)} %fusion.36, f32[256]{0:T(256)S(1)} %get-tuple-element.20, f32[256,1600]{0,1:T(8,128)} %copy-done, f16[256,1600]{0,1:T(8,128)(2,1)} %copy-done.1), kind=kLoop, calls=%fused_computation.10 | loop fusion | flops 2048000 | bytes 3278848 | tf_op jit(solution)/shard_map/convert_element_type | solution.py:129
  138.6 12.1 %gather_fusion = bf16[512,3072]{1,0:T(8,128)(2,1)} fusion(bf16[1600,3072]{1,0:T(8,128)(2,1)} %param.6, s32[1024]{0:T(1024)S(1)} %pad_clamp_fusion), kind=kCustom, calls=%fused_computation | custom fusion | bytes 6293504 | tf_op jit(solution)/shard_map/jit(_take)/gather | solution.py:136
  151.0 1.1 convert_reduce_fusion
  152.1 2.2 copy.79
  154.3 2.2 copy.80
  156.5 2.2 copy.81
  158.7 10.0 %subtract_multiply_fusion = f32[512,3072]{1,0:T(8,128)S(1)} fusion(bf16[1600,3072]{1,0:T(8,128)(2,1)} %param.6, f32[512]{0:T(512)S(1)} %convert_reduce_fusion, bf16[512,3072]{1,0:T(8,128)(2,1)} %gather_fusion, pred[512]{0:T(512)(128)(4,1)S(1)} %get-tuple-element.6, bf16[256,1600]{0,1:T(8,128)(2,1)} %copy.81, bf16[256,1600]{0,1:T(8,128)(2,1)} %divide_convert_fusion), kind=kOutput, calls=%fused_computation.7 | convolution fusion | flops 5044305920 | bytes 20908544 | tf_op jit(solution)/shard_map/dot_general | solution.py:137
  169.7 1.1 collective-permute-start.12
  170.9 2.2 collective-permute-start.11
  173.5 9.9 %collective-permute-done.12 = f16[2,4,16,3072]{3,2,0,1:T(8,128)(2,1)S(1)} collective-permute-done((f16[2,4,16,3072]{3,2,0,1:T(8,128)(2,1)S(1)}, f16[2,4,16,3072]{3,2,0,1:T(8,128)(2,1)S(1)}, u32[]{:S(2)}, u32[]{:S(2)}) %collective-permute-start.12) | collective-permute-done | bytes 786464 | tf_op jit(solution)/shard_map/ppermute | solution.py:23
  183.4 6.7 %collective-permute-done.11 = f16[2,4,16,3072]{3,2,0,1:T(8,128)(2,1)S(1)} collective-permute-done((f16[2,4,16,3072]{3,2,0,1:T(8,128)(2,1)S(1)}, f16[2,4,16,3072]{3,2,0,1:T(8,128)(2,1)S(1)}, u32[]{:S(2)}, u32[]{:S(2)}) %collective-permute-start.11) | collective-permute-done | bytes 786464 | tf_op jit(solution)/shard_map/ppermute | solution.py:23
  190.1 1.6 collective-permute-done.10
  193.0 2.0 collective-permute-start.15
  195.0 1.3 collective-permute-start.14
  196.3 16.1 %fusion = f32[1600,3072]{1,0:T(8,128)} fusion(bf16[512,3072]{1,0:T(8,128)(2,1)S(1)} %bitcast_negate_fusion, bf16[512,3072]{1,0:T(8,128)(2,1)} %bitcast.68, s32[1024]{0:T(1024)S(1)} %add_subtract_fusion), kind=kOutput, calls=%fused_computation.3 | convolution fusion | flops 10080550912 | bytes 25956352 | tf_op jit(solution)/shard_map/dot_general | solution.py:147
  213.2 11.9 %add_convert_fusion = bf16[1600,3072]{1,0:T(8,128)(2,1)} fusion(f32[1600,3072]{1,0:T(8,128)} %fusion, bf16[512,3072]{1,0:T(8,128)(2,1)S(1)} %bitcast.167, bf16[256,1600]{0,1:T(8,128)(2,1)S(1)} %copy-done.3, bf16[256,1600]{0,1:T(8,128)(2,1)} %divide_convert_fusion), kind=kOutput, calls=%fused_computation.1 | convolution fusion | flops 5046272000 | bytes 34275328 | tf_op jit(solution)/shard_map/dot_general | solution.py:146
  (91 shorter events, 19.5 us)
Async XLA Ops:
  0.6 4.9 %collective-permute-start.17 = (bf16[16,3072]{1,0:T(8,128)(2,1)}, bf16[16,3072]{1,0:T(8,128)(2,1)S(1)}, u32[]{:S(2)}, u32[]{:S(2)}) collective-permute-start(bf16[16,3072]{1,0:T(8,128)(2,1)} %param.7), channel_id=1, source_target_pairs={{0,16},{1,17},{2,18},{3,19},{4,20},{5,21},{6,22},{7,23},{8,24},{9,... | collective-permute-start | bytes 294920 | tf_op jit(solution)/shard_map/ppermute | solution.py:23
  4.1 11.2 %collective-permute-start = (bf16[16,3200]{1,0:T(8,128)(2,1)S(1)}, bf16[16,3200]{1,0:T(8,128)(2,1)S(1)}, u32[]{:S(2)}, u32[]{:S(2)}) collective-permute-start(bf16[16,3200]{1,0:T(8,128)(2,1)S(1)} %get-tuple-element.19), channel_id=1, source_target_pairs={{0,16},{1,17},{2,18},{3,19},{4,20},{5,21},{6,22},{7,23},{8,24},{9,... | collective-permute-start | bytes 307208 | tf_op jit(solution)/shard_map/ppermute | solution.py:23
  6.5 14.1 %collective-permute-start.20 = (bf16[2,16,3072]{2,1,0:T(8,128)(2,1)S(1)}, bf16[2,16,3072]{2,1,0:T(8,128)(2,1)S(1)}, u32[]{:S(2)}, u32[]{:S(2)}) collective-permute-start(bf16[2,16,3072]{2,1,0:T(8,128)(2,1)S(1)} %maximum_select_fusion.3), channel_id=1, source_target_pairs={{0,64},{1,9},{2,66},{3,11},{4,68},{5,13},{6,70},{7,15},{8,72},{9,1... | collective-permute-start | bytes 589832 | tf_op jit(solution)/shard_map/ppermute | solution.py:23
  10.6 9.4 %collective-permute-start.19 = (bf16[2,16,3072]{2,1,0:T(8,128)(2,1)S(1)}, bf16[2,16,3072]{2,1,0:T(8,128)(2,1)S(1)}, u32[]{:S(2)}, u32[]{:S(2)}) collective-permute-start(bf16[2,16,3072]{2,1,0:T(8,128)(2,1)S(1)} %maximum_select_fusion.3), channel_id=1, source_target_pairs={{0,96},{1,13},{2,98},{3,15},{4,100},{5,1},{6,102},{7,3},{8,104},{9... | collective-permute-start | bytes 589832 | tf_op jit(solution)/shard_map/ppermute | solution.py:23
  11.3 7.9 %collective-permute-start.18 = (bf16[2,16,3072]{2,1,0:T(8,128)(2,1)S(1)}, bf16[2,16,3072]{2,1,0:T(8,128)(2,1)S(1)}, u32[]{:S(2)}, u32[]{:S(2)}) collective-permute-start(bf16[2,16,3072]{2,1,0:T(8,128)(2,1)S(1)} %maximum_select_fusion.3), channel_id=1, source_target_pairs={{0,32},{1,5},{2,34},{3,7},{4,36},{5,9},{6,38},{7,11},{8,40},{9,13}... | collective-permute-start | bytes 589832 | tf_op jit(solution)/shard_map/ppermute | solution.py:23
  15.3 21.5 %collective-permute-start.3 = (bf16[2,16,3200]{2,1,0:T(8,128)(2,1)S(1)}, bf16[2,16,3200]{2,1,0:T(8,128)(2,1)S(1)}, u32[]{:S(2)}, u32[]{:S(2)}) collective-permute-start(bf16[2,16,3200]{2,1,0:T(8,128)(2,1)S(1)} %maximum_select_fusion.1), channel_id=1, source_target_pairs={{0,64},{1,9},{2,66},{3,11},{4,68},{5,13},{6,70},{7,15},{8,72},{9,1... | collective-permute-start | bytes 614408 | tf_op jit(solution)/shard_map/ppermute | solution.py:23
  16.4 20.3 %collective-permute-start.2 = (bf16[2,16,3200]{2,1,0:T(8,128)(2,1)S(1)}, bf16[2,16,3200]{2,1,0:T(8,128)(2,1)S(1)}, u32[]{:S(2)}, u32[]{:S(2)}) collective-permute-start(bf16[2,16,3200]{2,1,0:T(8,128)(2,1)S(1)} %maximum_select_fusion.1), channel_id=1, source_target_pairs={{0,96},{1,13},{2,98},{3,15},{4,100},{5,1},{6,102},{7,3},{8,104},{9... | collective-permute-start | bytes 614408 | tf_op jit(solution)/shard_map/ppermute | solution.py:23
  19.2 15.5 %collective-permute-start.1 = (bf16[2,16,3200]{2,1,0:T(8,128)(2,1)S(1)}, bf16[2,16,3200]{2,1,0:T(8,128)(2,1)S(1)}, u32[]{:S(2)}, u32[]{:S(2)}) collective-permute-start(bf16[2,16,3200]{2,1,0:T(8,128)(2,1)S(1)} %maximum_select_fusion.1), channel_id=1, source_target_pairs={{0,32},{1,5},{2,34},{3,7},{4,36},{5,9},{6,38},{7,11},{8,40},{9,13}... | collective-permute-start | bytes 614408 | tf_op jit(solution)/shard_map/ppermute | solution.py:23
  21.3 77.6 %collective-permute-start.23 = (bf16[2,4,16,3072]{3,2,1,0:T(8,128)(2,1)}, bf16[2,4,16,3072]{3,2,1,0:T(8,128)(2,1)}, u32[]{:S(2)}, u32[]{:S(2)}) collective-permute-start(bf16[2,4,16,3072]{3,2,1,0:T(8,128)(2,1)} %bitcast_dynamic-update-slice_fusion.9), channel_id=1, source_target_pairs={{0,8},{1,65},{2,10},{3,67},{4,12},{5,69},{6,14},{7,71},{8,0},{9,73... | collective-permute-start | bytes 2359304 | tf_op jit(solution)/shard_map/ppermute | solution.py:23
  24.3 52.9 %collective-permute-start.22 = (bf16[2,4,16,3072]{3,2,1,0:T(8,128)(2,1)}, bf16[2,4,16,3072]{3,2,1,0:T(8,128)(2,1)S(1)}, u32[]{:S(2)}, u32[]{:S(2)}) collective-permute-start(bf16[2,4,16,3072]{3,2,1,0:T(8,128)(2,1)} %bitcast_dynamic-update-slice_fusion.9), channel_id=1, source_target_pairs={{0,12},{1,97},{2,14},{3,99},{4,0},{5,101},{6,2},{7,103},{8,4},{9,1... | collective-permute-start | bytes 2359304 | tf_op jit(solution)/shard_map/ppermute | solution.py:23
  34.7 41.6 %collective-permute-start.21 = (bf16[2,4,16,3072]{3,2,1,0:T(8,128)(2,1)}, bf16[2,4,16,3072]{3,2,1,0:T(8,128)(2,1)S(1)}, u32[]{:S(2)}, u32[]{:S(2)}) collective-permute-start(bf16[2,4,16,3072]{3,2,1,0:T(8,128)(2,1)} %bitcast_dynamic-update-slice_fusion.9), channel_id=1, source_target_pairs={{0,4},{1,33},{2,6},{3,35},{4,8},{5,37},{6,10},{7,39},{8,12},{9,41}... | collective-permute-start | bytes 2359304 | tf_op jit(solution)/shard_map/ppermute | solution.py:23
  36.8 20.1 %collective-permute-start.4 = (bf16[2,4,16,3200]{3,2,1,0:T(8,128)(2,1)S(1)}, bf16[2,4,16,3200]{3,2,1,0:T(8,128)(2,1)S(1)}, u32[]{:S(2)}, u32[]{:S(2)}) collective-permute-start(bf16[2,4,16,3200]{3,2,1,0:T(8,128)(2,1)S(1)} %bitcast_dynamic-update-slice_fusion.6), channel_id=1, source_target_pairs={{0,4},{1,33},{2,6},{3,35},{4,8},{5,37},{6,10},{7,39},{8,12},{9,41}... | collective-permute-start | bytes 2457608 | tf_op jit(solution)/shard_map/ppermute | solution.py:23
  38.4 34.8 %slice-start = ((s8[9830400]{0:T(1024)(128)(4,1)}), s8[4194304]{0:T(1024)(128)(4,1)S(1)}, s32[]{:S(2)}) async-start(s8[9830400]{0:T(1024)(128)(4,1)} %bitcast.165), calls=%async_computation.1 | async-start | bytes 8388608
  42.9 30.3 %slice-start.1 = ((s8[9830400]{0:T(1024)(128)(4,1)}), s8[4194304]{0:T(1024)(128)(4,1)S(1)}, s32[]{:S(2)}) async-start(s8[9830400]{0:T(1024)(128)(4,1)} %bitcast.165), calls=%async_computation.2 | async-start | bytes 8388608
  42.9 16.4 %collective-permute-start.5 = (bf16[2,4,16,3200]{3,2,1,0:T(8,128)(2,1)S(1)}, bf16[2,4,16,3200]{3,2,1,0:T(8,128)(2,1)S(1)}, u32[]{:S(2)}, u32[]{:S(2)}) collective-permute-start(bf16[2,4,16,3200]{3,2,1,0:T(8,128)(2,1)S(1)} %bitcast_dynamic-update-slice_fusion.6), channel_id=1, source_target_pairs={{0,12},{1,97},{2,14},{3,99},{4,0},{5,101},{6,2},{7,103},{8,4},{9,1... | collective-permute-start | bytes 2457608 | tf_op jit(solution)/shard_map/ppermute | solution.py:23
  56.9 2.4 %copy-start.4 = (bf16[2,4,16,3200]{3,2,1,0:T(8,128)(2,1)}, bf16[2,4,16,3200]{3,2,1,0:T(8,128)(2,1)S(1)}, u32[]{:S(2)}) copy-start(bf16[2,4,16,3200]{3,2,1,0:T(8,128)(2,1)S(1)} %collective-permute-done.4) | copy-start | bytes 2457604
  56.9 13.8 %collective-permute-start.6 = (bf16[2,4,16,3200]{3,2,1,0:T(8,128)(2,1)S(1)}, bf16[2,4,16,3200]{3,2,1,0:T(8,128)(2,1)S(1)}, u32[]{:S(2)}, u32[]{:S(2)}) collective-permute-start(bf16[2,4,16,3200]{3,2,1,0:T(8,128)(2,1)S(1)} %bitcast_dynamic-update-slice_fusion.6), channel_id=1, source_target_pairs={{0,8},{1,65},{2,10},{3,67},{4,12},{5,69},{6,14},{7,71},{8,0},{9,73... | collective-permute-start | bytes 2457608 | tf_op jit(solution)/shard_map/ppermute | solution.py:23
  59.4 11.4 %copy-start.5 = (bf16[2,4,16,3200]{3,2,1,0:T(8,128)(2,1)}, bf16[2,4,16,3200]{3,2,1,0:T(8,128)(2,1)S(1)}, u32[]{:S(2)}) copy-start(bf16[2,4,16,3200]{3,2,1,0:T(8,128)(2,1)S(1)} %collective-permute-done.5) | copy-start | bytes 2457604
  59.4 13.7 %slice-start.2 = ((s8[9830400]{0:T(1024)(128)(4,1)}), s8[1441792]{0:T(1024)(128)(4,1)S(1)}, s32[]{:S(2)}) async-start(s8[9830400]{0:T(1024)(128)(4,1)} %bitcast.165), calls=%async_computation.3 | async-start | bytes 2883584
  70.8 0.9 copy-start.6
  76.0 3.9 %collective-permute-start.7 = (f32[256,1600]{0,1:T(8,128)S(1)}, f32[256,1600]{0,1:T(8,128)}, u32[]{:S(2)}, u32[]{:S(2)}) collective-permute-start(f32[256,1600]{0,1:T(8,128)S(1)} %fusion.49), channel_id=1, source_target_pairs={{0,1},{1,0},{2,3},{3,2},{4,5},{5,4},{6,7},{7,6},{8,9},{9,8},{10,11... | collective-permute-start | bytes 4915208 | tf_op jit(solution)/shard_map/ppermute | solution.py:23
  95.6 22.6 %copy-start = (f32[256,1600]{0,1:T(8,128)}, f32[256,1600]{0,1:T(8,128)S(1)}, u32[]{:S(2)}) copy-start(f32[256,1600]{0,1:T(8,128)S(1)} %get-tuple-element.5) | copy-start | bytes 4915204
  95.6 21.9 %collective-permute-start.8 = (f16[256,1600]{0,1:T(8,128)(2,1)S(1)}, f16[256,1600]{0,1:T(8,128)(2,1)S(1)}, u32[]{:S(2)}, u32[]{:S(2)}) collective-permute-start(f16[256,1600]{0,1:T(8,128)(2,1)S(1)} %get-tuple-element.4), channel_id=1, source_target_pairs={{0,2},{1,3},{2,0},{3,1},{4,6},{5,7},{6,4},{7,5},{8,10},{9,11},{10,... | collective-permute-start | bytes 2457608 | tf_op jit(solution)/shard_map/ppermute | solution.py:23
  117.5 0.9 copy-start.1
  119.1 14.4 %all-to-all-start = ((f32[32,2,256]{2,1,0:T(2,128)}), f32[32,2,256]{2,1,0:T(2,128)}, u32[]{:S(2)}, u32[]{:S(2)}) async-start(f32[32,2,256]{2,1,0:T(2,128)} %broadcast_in_dim.95), calls=%async_computation | async-start | bytes 131072 | tf_op jit(solution)/shard_map/all_to_all | solution.py:126
  137.4 14.7 %collective-permute-start.9 = (bf16[256,1600]{0,1:T(8,128)(2,1)}, bf16[256,1600]{0,1:T(8,128)(2,1)}, u32[]{:S(2)}, u32[]{:S(2)}) collective-permute-start(bf16[256,1600]{0,1:T(8,128)(2,1)} %divide_convert_fusion), channel_id=1, source_target_pairs={{0,1},{1,0},{2,3},{3,2},{4,5},{5,4},{6,7},{7,6},{8,9},{9,8},{10,11... | collective-permute-start | bytes 2457608 | tf_op jit(solution)/shard_map/ppermute | solution.py:23
  137.7 0.7 copy-start.2
  169.7 13.7 %collective-permute-start.12 = (f16[2,4,16,3072]{3,2,0,1:T(8,128)(2,1)S(1)}, f16[2,4,16,3072]{3,2,0,1:T(8,128)(2,1)S(1)}, u32[]{:S(2)}, u32[]{:S(2)}) collective-permute-start(f16[2,4,16,3072]{3,2,0,1:T(8,128)(2,1)S(1)} %fusion.9), channel_id=1, source_target_pairs={{0,8},{1,65},{2,10},{3,67},{4,12},{5,69},{6,14},{7,71},{8,0},{9,73... | collective-permute-start | bytes 2359304 | tf_op jit(solution)/shard_map/ppermute | solution.py:23
  170.9 19.3 %collective-permute-start.11 = (f16[2,4,16,3072]{3,2,0,1:T(8,128)(2,1)S(1)}, f16[2,4,16,3072]{3,2,0,1:T(8,128)(2,1)S(1)}, u32[]{:S(2)}, u32[]{:S(2)}) collective-permute-start(f16[2,4,16,3072]{3,2,0,1:T(8,128)(2,1)S(1)} %fusion.8), channel_id=1, source_target_pairs={{0,12},{1,97},{2,14},{3,99},{4,0},{5,101},{6,2},{7,103},{8,4},{9,1... | collective-permute-start | bytes 2359304 | tf_op jit(solution)/shard_map/ppermute | solution.py:23
  173.1 18.7 %collective-permute-start.10 = (f16[2,4,16,3072]{3,2,0,1:T(8,128)(2,1)S(1)}, f16[2,4,16,3072]{3,2,0,1:T(8,128)(2,1)S(1)}, u32[]{:S(2)}, u32[]{:S(2)}) collective-permute-start(f16[2,4,16,3072]{3,2,0,1:T(8,128)(2,1)S(1)} %fusion.7), channel_id=1, source_target_pairs={{0,4},{1,33},{2,6},{3,35},{4,8},{5,37},{6,10},{7,39},{8,12},{9,41}... | collective-permute-start | bytes 2359304 | tf_op jit(solution)/shard_map/ppermute | solution.py:23
  192.3 20.1 %collective-permute-start.13 = (f16[2,16,3072]{2,1,0:T(8,128)(2,1)S(1)}, f16[2,16,3072]{2,1,0:T(8,128)(2,1)S(1)}, u32[]{:S(2)}, u32[]{:S(2)}) collective-permute-start(f16[2,16,3072]{2,1,0:T(8,128)(2,1)S(1)} %get-tuple-element.14), channel_id=1, source_target_pairs={{0,32},{1,5},{2,34},{3,7},{4,36},{5,9},{6,38},{7,11},{8,40},{9,13}... | collective-permute-start | bytes 589832 | tf_op jit(solution)/shard_map/ppermute | solution.py:23
  193.0 19.4 %collective-permute-start.15 = (f16[2,16,3072]{2,1,0:T(8,128)(2,1)S(1)}, f16[2,16,3072]{2,1,0:T(8,128)(2,1)S(1)}, u32[]{:S(2)}, u32[]{:S(2)}) collective-permute-start(f16[2,16,3072]{2,1,0:T(8,128)(2,1)S(1)} %get-tuple-element.15), channel_id=1, source_target_pairs={{0,64},{1,9},{2,66},{3,11},{4,68},{5,13},{6,70},{7,15},{8,72},{9,1... | collective-permute-start | bytes 589832 | tf_op jit(solution)/shard_map/ppermute | solution.py:23
  195.0 17.4 %collective-permute-start.14 = (f16[2,16,3072]{2,1,0:T(8,128)(2,1)S(1)}, f16[2,16,3072]{2,1,0:T(8,128)(2,1)S(1)}, u32[]{:S(2)}, u32[]{:S(2)}) collective-permute-start(f16[2,16,3072]{2,1,0:T(8,128)(2,1)S(1)} %get-tuple-element.16), channel_id=1, source_target_pairs={{0,96},{1,13},{2,98},{3,15},{4,100},{5,1},{6,102},{7,3},{8,104},{9... | collective-permute-start | bytes 589832 | tf_op jit(solution)/shard_map/ppermute | solution.py:23
  196.3 16.9 %copy-start.3 = (bf16[256,1600]{0,1:T(8,128)(2,1)S(1)}, bf16[256,1600]{0,1:T(8,128)(2,1)}, u32[]{:S(2)}) copy-start(bf16[256,1600]{0,1:T(8,128)(2,1)} %copy.81) | copy-start | bytes 2457604
  212.5 12.6 %collective-permute-start.16 = (f16[16,3072]{1,0:T(8,128)(2,1)S(1)}, f16[16,3072]{1,0:T(8,128)(2,1)S(1)}, u32[]{:S(2)}, u32[]{:S(2)}) collective-permute-start(f16[16,3072]{1,0:T(8,128)(2,1)S(1)} %fusion.28), channel_id=1, source_target_pairs={{0,16},{1,17},{2,18},{3,19},{4,20},{5,21},{6,22},{7,23},{8,24},{9,... | collective-permute-start | bytes 294920 | tf_op jit(solution)/shard_map/ppermute | solution.py:23

commit v2 on v1

v2 whole, which is shorter than its diff:
```python
import functools

import jax
import jax.numpy as jnp
from jax import lax
from jax.experimental import pallas as pl
from jax.experimental.pallas import tpu as pltpu
from jax.sharding import PartitionSpec as P

BF16, F16, F32, I32 = jnp.bfloat16, jnp.float16, jnp.float32, jnp.int32
BOTH = ("section", "tensor")
SCALE = 16384.0
VMEM = 24 * 1024 * 1024
LARGE = 50 * 1024 * 1024
ROWS = 16
CHUNK = 256
TOKENS = 512
MANY = 128
ANY = pl.BlockSpec(memory_space=pl.ANY)
NEAR = pl.BlockSpec(memory_space=pltpu.VMEM)


def linear(z, yl, x, yh, c):
    return (((z * 2 + yl) * 4 + x) * 2 + yh) * 2 + c


def permute(value, move):
    pairs = []
    for z in range(4):
        for yl in range(2):
            for x in range(4):
                for yh in range(2):
                    for c in range(2):
                        pairs.append((linear(z, yl, x, yh, c), linear(*move(z, yl, x, yh, c))))
    return lax.ppermute(value, BOTH, pairs)


def swap_y(value):
    return permute(value, lambda z, yl, x, yh, c: (z, 1 - yl, x, yh, c))


def swap_core(value):
    return permute(value, lambda z, yl, x, yh, c: (z, yl, x, yh, 1 - c))


def swap_half(value):
    return permute(value, lambda z, yl, x, yh, c: (z, yl, x, 1 - yh, c))


def ring_a(value, k):
    return permute(
        value,
        lambda z, yl, x, yh, c: ((z + k) % 4, yl, x, yh, c) if c == 0 else (z, yl, (x + k) % 4, yh, c),
    )


def ring_b(value, k):
    return permute(
        value,
        lambda z, yl, x, yh, c: (z, yl, (x + k) % 4, yh, c) if c == 0 else ((z + k) % 4, yl, x, yh, c),
    )


def gather_rows(own, bottom):
    both = jnp.stack([own, bottom])
    lines = jnp.stack([both] + [ring_a(both, k) for k in (1, 2, 3)], axis=1)
    line, bottom = lines[0], lines[1]
    other = swap_y(line)
    later = jnp.where(other[0, 0, -128] >= 0, line, 0)
    mine = [line, ring_b(line, 1), ring_b(later, 2), ring_b(line, 3)]
    chunks = [mine, [other] + [ring_b(other, k) for k in (1, 2, 3)]]
    return chunks, (bottom, swap_y(bottom))


def gather_rest(lines, ready):
    line = jnp.where(ready, jnp.concatenate(lines), 0)
    parts = [line] + [ring_b(line, k) for k in (1, 2, 3)]
    return [part.reshape(8 * ROWS, part.shape[-1]) for part in parts]


def ring_sum(total, shift):
    total = total.astype(F16)
    parts = [shift(total[k], -k).astype(F32) for k in (1, 2, 3)]
    return total[0].astype(F32) + parts[0] + parts[1] + parts[2]


ORDER = [(2 * m + par, j) for par in range(2) for m in range(2) for j in range(4)]


def fetch_rows(core, pieces, rows, first, done):
    width = rows.shape[1]

    def start(n, piece, j):
        source = piece.at[j, :, pl.ds(0, width)]
        pltpu.make_async_copy(source, rows.at[pl.ds(first + ROWS * n, ROWS), :], done.at[n]).start()

    @pl.when(core == 0)
    def _():
        for n, (i, j) in enumerate(ORDER):
            start(n, pieces[i], j)

    @pl.when(core != 0)
    def _():
        for n, (i, j) in enumerate(ORDER):
            start(n, pieces[j], i)


def await_rows(pieces, rows, first, done):
    width = rows.shape[1]
    for n in range(len(ORDER)):
        source = pieces[0].at[0, :, pl.ds(0, width)]
        pltpu.make_async_copy(source, rows.at[pl.ds(first + ROWS * n, ROWS), :], done.at[n]).wait()


def logits_kernel(flags, *refs):
    pieces, (table, kept, sent, out, rows, turned, tiles, done, left, arrived) = refs[:8], refs[8:]
    step, half = table.shape[0] // 4, CHUNK // 2
    parts = [pl.ds(step * n, step) for n in range(4)]
    copies = [pltpu.make_async_copy(table.at[p, :], tiles.at[p, :], arrived.at[n]) for n, p in enumerate(parts)]
    for c in range(2):
        fetch_rows(flags[0], pieces[4 * c : 4 * c + 4], rows, CHUNK * c, done.at[c])
    for tile in copies:
        tile.start()
    for c in range(2):
        await_rows(pieces[4 * c : 4 * c + 4], rows, CHUNK * c, done.at[c])
    copy = pltpu.make_async_copy(rows, out, left.at[0])
    copy.start()
    turned[...] = rows[...].T
    even = flags[1] == 0
    for n in range(4):
        copies[n].wait()
        part = slice(step * n, step * (n + 1))
        product = jnp.dot(tiles[part, :], turned[...], preferred_element_type=F32)
        for c in range(2):
            lanes = slice(half * c, half * (c + 1))
            low = product[:, CHUNK * c : CHUNK * c + half]
            high = product[:, CHUNK * c + half : CHUNK * (c + 1)]
            kept[part, lanes] = jnp.where(even, low, high)
            sent[part, lanes] = jnp.where(even, high, low)
    copy.wait()


def logits_part(flags, chunks, table):
    vocab, width = table.shape
    return pl.pallas_call(
        logits_kernel,
        grid_spec=pltpu.PrefetchScalarGridSpec(
            num_scalar_prefetch=1,
            grid=(),
            in_specs=[ANY] * 9,
            out_specs=[NEAR, NEAR, ANY],
            scratch_shapes=[
                pltpu.VMEM((TOKENS, width), BF16),
                pltpu.VMEM((width, TOKENS), BF16),
                pltpu.VMEM((vocab, width), BF16),
                pltpu.SemaphoreType.DMA((2, len(ORDER))),
                pltpu.SemaphoreType.DMA((1,)),
                pltpu.SemaphoreType.DMA((4,)),
            ],
        ),
        out_shape=[jax.ShapeDtypeStruct((vocab, CHUNK), F32)] * 2 + [jax.ShapeDtypeStruct((TOKENS, width), BF16)],
        compiler_params=pltpu.CompilerParams(vmem_limit_bytes=LARGE),
        cost_estimate=pl.CostEstimate(flops=2 * TOKENS * vocab * width, bytes_accessed=16 << 20, transcendentals=0),
    )(flags, *chunks[0], *chunks[1], table)


def turning(flags):
    place = lax.broadcasted_iota(I32, (CHUNK, CHUNK), 0)
    step = lax.broadcasted_iota(I32, (CHUNK, CHUNK), 1)
    y = (step // 128 + flags[2]) % 2
    x = (flags[3] + 2 - step // 64 % 2) % 2
    z = (flags[4] + 4 - step // 16 % 4) % 4
    return (place == y * 128 + x * 64 + z * 16 + step % 16).astype(F32)


def turn(flags, rows):
    both = jnp.concatenate(rows + [jnp.zeros((8 - len(rows), CHUNK), F32)], axis=0)
    return jnp.dot(both, turning(flags), precision=lax.Precision.HIGHEST, preferred_element_type=F32)


def stats_kernel(flags, logits, after, stats):
    del after
    top = jnp.max(logits[...], axis=0, keepdims=True)
    total = jnp.sum(jnp.exp(logits[...] - top), axis=0, keepdims=True)
    placed = turn(flags, [top, total])
    for n in range(32):
        stats[n] = placed[0:2]


def stats_part(flags, logits, after):
    return pl.pallas_call(
        stats_kernel,
        grid_spec=pltpu.PrefetchScalarGridSpec(
            num_scalar_prefetch=1, grid=(), in_specs=[NEAR, ANY], out_specs=NEAR
        ),
        out_shape=jax.ShapeDtypeStruct((32, 2, CHUNK), F32),
        compiler_params=pltpu.CompilerParams(vmem_limit_bytes=VMEM),
        cost_estimate=pl.CostEstimate(flops=1 << 20, bytes_accessed=2 << 20, transcendentals=logits.size),
    )(flags, logits, after)


def probs_kernel(flags, stats, logits, after0, after1, after2, probs):
    del after0, after1, after2
    top = jnp.max(stats[:, 0, :], axis=0, keepdims=True)
    total = jnp.sum(stats[:, 1, :] * jnp.exp(stats[:, 0, :] - top), axis=0, keepdims=True)
    both = turn(flags, [top, total])
    probs[...] = (jnp.exp(logits[...] - both[0:1]) / both[1:2]).astype(BF16)


def probs_part(flags, stats, logits, after):
    return pl.pallas_call(
        probs_kernel,
        grid_spec=pltpu.PrefetchScalarGridSpec(
            num_scalar_prefetch=1, grid=(), in_specs=[NEAR, NEAR, ANY, ANY, ANY], out_specs=NEAR
        ),
        out_shape=jax.ShapeDtypeStruct(logits.shape, BF16),
        compiler_params=pltpu.CompilerParams(vmem_limit_bytes=VMEM),
        cost_estimate=pl.CostEstimate(flops=1 << 20, bytes_accessed=3 << 20, transcendentals=logits.size),
    )(flags, stats, logits, *after)


def ranks(by_lane, by_row, vocab):
    count = by_row.shape[0]
    lane_in = ((by_lane >= 0) & (by_lane < vocab)).astype(F32)
    row_in = ((by_row >= 0) & (by_row < vocab)).astype(F32)
    row = lax.broadcasted_iota(I32, (count, count), 0)
    lane = lax.broadcasted_iota(I32, (count, count), 1)
    lane_rank = jnp.sum(jnp.where(row < lane, row_in, 0.0), axis=0, keepdims=True).astype(I32)
    row_rank = jnp.sum(jnp.where(lane < row, lane_in, 0.0), axis=1, keepdims=True).astype(I32)
    return (
        jnp.where(lane_in > 0.0, lane_rank, -1),
        jnp.where(row_in > 0.0, row_rank, -1),
        jnp.sum(lane_in).astype(I32),
    )


def write_blocks(core, value, out, columns=slice(None), less=None):
    def write(c, n, i, j):
        rows = value[CHUNK * c + ROWS * n : CHUNK * c + ROWS * (n + 1)]
        if less is not None:
            rows = (rows - less[i, c, j, :, columns].astype(F32)) * SCALE
        out[i, c, j, :, columns] = rows

    @pl.when(core == 0)
    def _():
        for c in range(2):
            for n, (i, j) in enumerate(ORDER):
                write(c, n, i, j)

    @pl.when(core != 0)
    def _():
        for c in range(2):
            for n, (i, j) in enumerate(ORDER):
                write(c, n, j, i)


def target_kernel(flags, table, by_lane, by_row, after, out, lane_rank, row_rank, rows, tokens, hits):
    del after
    vocab = table.shape[0]

    def picks(first):
        slot = first + lax.broadcasted_iota(I32, (MANY, TOKENS), 0)
        found = jnp.sum(jnp.where(lane_rank[...] == slot, by_lane[...], 0), axis=1, keepdims=True)
        rows = (lax.broadcasted_iota(I32, (MANY, vocab), 1) == found).astype(F32).astype(BF16)
        slot = first + lax.broadcasted_iota(I32, (TOKENS, MANY), 1)
        return rows, (row_rank[...] == slot).astype(F32).astype(BF16)

    lane, row, count = ranks(by_lane[...], by_row[...], vocab)
    lane_rank[...] = lane
    row_rank[...] = row
    hits[0] = count
    rows[...], tokens[...] = picks(0)

    @pl.loop(0, table.shape[1] // 512)
    def _(n):
        columns = pl.ds(pl.multiple_of(n * 512, 512), 512)

        def spread_rows(rows, tokens):
            few = jnp.dot(rows, table[:, columns], preferred_element_type=F32).astype(BF16)
            return jnp.dot(tokens, few, preferred_element_type=F32)

        value = spread_rows(rows[...], tokens[...])
        write_blocks(flags[0], value.astype(BF16), out, columns)

        @pl.when(hits[0] > MANY)
        def _():
            def more(n, total):
                return total + spread_rows(*picks(n * MANY))

            value = lax.fori_loop(1, (hits[0] + MANY - 1) // MANY, more, spread_rows(rows[...], tokens[...]))
            write_blocks(flags[0], value.astype(BF16), out, columns)


def target_rows(flags, table, wanted, after):
    vocab, width = table.shape
    return pl.pallas_call(
        target_kernel,
        grid_spec=pltpu.PrefetchScalarGridSpec(
            num_scalar_prefetch=1,
            grid=(),
            in_specs=[NEAR, NEAR, NEAR, ANY],
            out_specs=NEAR,
            scratch_shapes=[
                pltpu.VMEM((1, TOKENS), I32),
                pltpu.VMEM((TOKENS, 1), I32),
                pltpu.VMEM((MANY, vocab), BF16),
                pltpu.VMEM((TOKENS, MANY), BF16),
                pltpu.SMEM((1,), I32),
            ],
        ),
        out_shape=jax.ShapeDtypeStruct((4, 2, 4, ROWS, width), BF16),
        compiler_params=pltpu.CompilerParams(vmem_limit_bytes=VMEM),
        cost_estimate=pl.CostEstimate(flops=512 * vocab * width, bytes_accessed=14 << 20, transcendentals=0),
    )(flags, table, wanted[None, :], wanted[:, None], after)


def input_kernel(flags, kept, got, table, picked, out, both, turned, left, done):
    half, step = CHUNK // 2, 512
    for n in range(2):
        mine = pl.multiple_of(n * CHUNK + flags[1] * half, half)
        other = pl.multiple_of(n * CHUNK + (1 - flags[1]) * half, half)
        lanes = slice(half * n, half * (n + 1))
        turned[:, pl.ds(mine, half)] = kept[:, lanes]
        turned[:, pl.ds(other, half)] = got[:, lanes]
    copy = pltpu.make_async_copy(turned, both, done.at[0])
    copy.start()
    left[...] = turned[...].T

    @pl.loop(0, table.shape[1] // step)
    def _(n):
        columns = pl.ds(pl.multiple_of(n * step, step), step)
        value = jnp.dot(left[...], table[:, columns], preferred_element_type=F32)
        write_blocks(flags[0], value, out, columns, picked)

    copy.wait()


def input_part(flags, table, kept, got, picked):
    vocab, width = table.shape
    return pl.pallas_call(
        input_kernel,
        grid_spec=pltpu.PrefetchScalarGridSpec(
            num_scalar_prefetch=1,
            grid=(),
            in_specs=[NEAR, NEAR, NEAR, NEAR],
            out_specs=[NEAR, ANY],
            scratch_shapes=[
                pltpu.VMEM((vocab, TOKENS), BF16),
                pltpu.VMEM((TOKENS, vocab), BF16),
                pltpu.SemaphoreType.DMA((1,)),
            ],
        ),
        out_shape=[
            jax.ShapeDtypeStruct((4, 2, 4, ROWS, width), F32),
            jax.ShapeDtypeStruct((vocab, TOKENS), BF16),
        ],
        compiler_params=pltpu.CompilerParams(vmem_limit_bytes=VMEM),
        cost_estimate=pl.CostEstimate(flops=1024 * vocab * width, bytes_accessed=16 << 20, transcendentals=0),
    )(flags, kept, got, table, picked)


def lookup_picks(first, vocab, lane_rank, row_rank, by_row):
    slot = first + lax.broadcasted_iota(I32, (MANY, 2 * TOKENS), 0)
    source = lax.broadcasted_iota(I32, (MANY, 2 * TOKENS), 1)
    sign = jnp.where(source < TOKENS, -1.0, 1.0)
    lie = jnp.where(lane_rank == slot, sign, 0.0).astype(BF16)
    slot = first + lax.broadcasted_iota(I32, (2 * TOKENS, MANY), 1)
    found = jnp.sum(jnp.where(row_rank == slot, by_row, 0), axis=0, keepdims=True)
    go = (lax.broadcasted_iota(I32, (vocab, MANY), 0) == found).astype(F32).astype(BF16)
    return lie, go


def lookup_kernel(flags, rows, b0, b1, b2, b3, c0, c1, c2, c3, near, far, few, go, lane_rank, row_rank, by_row, lie):
    @pl.when(pl.program_id(0) == 0)
    def _():
        vocab = go.shape[0]
        codes = [c[...].astype(F32) for c in (c0, c1, c2, c3)]
        lanes = [c.T for c in codes]
        lanes = [(c[0:1, :] * 256.0 + c[1:2, :]).astype(I32) - flags[5] for c in lanes]
        by_lane = jnp.concatenate([near[...]] + lanes, axis=1)
        by_row[0:TOKENS, :] = far[...]
        for n, c in enumerate(codes):
            ids = (c[:, 0:1] * 256.0 + c[:, 1:2]).astype(I32) - flags[5]
            by_row[TOKENS + 8 * ROWS * n : TOKENS + 8 * ROWS * (n + 1), :] = ids
        lane, row, _ = ranks(by_lane, by_row[...], vocab)
        lane_rank[...] = lane
        row_rank[...] = row
        lie[...], go[...] = lookup_picks(0, vocab, lane, row, by_row[...])

    few[...] = lookup_sum(lie[...], rows, (b0, b1, b2, b3)).astype(BF16)


def lookup_sum(lie, rows, bottom):
    total = 0.0
    first = 0
    for part in (rows, *bottom):
        total = total + jnp.dot(lie[:, first : first + part.shape[0]], part[...], preferred_element_type=F32)
        first += part.shape[0]
    return total


def lookup_rows(flags, rows, bottom, wanted, vocab):
    width = rows.shape[1]
    step = 1024 if width % 1024 == 0 else 512
    lane = pl.BlockSpec((1, 2 * TOKENS), lambda n, s: (0, 0))
    row = pl.BlockSpec((2 * TOKENS, 1), lambda n, s: (0, 0))
    return pl.pallas_call(
        lookup_kernel,
        grid_spec=pltpu.PrefetchScalarGridSpec(
            num_scalar_prefetch=1,
            grid=(width // step,),
            in_specs=[pl.BlockSpec((TOKENS, step), lambda n, s: (0, n))]
            + [pl.BlockSpec((8 * ROWS, step), lambda n, s: (0, n))] * 4
            + [pl.BlockSpec((8 * ROWS, 128), lambda n, s: (0, width // 128))] * 4
            + [pl.BlockSpec((1, TOKENS), lambda n, s: (0, 0)), pl.BlockSpec((TOKENS, 1), lambda n, s: (0, 0))],
            out_specs=[
                pl.BlockSpec((MANY, step), lambda n, s: (0, n)),
                pl.BlockSpec((vocab, MANY), lambda n, s: (0, 0)),
                lane,
                row,
                row,
            ],
            scratch_shapes=[pltpu.VMEM((MANY, 2 * TOKENS), BF16)],
        ),
        out_shape=[
            jax.ShapeDtypeStruct((MANY, width), BF16),
            jax.ShapeDtypeStruct((vocab, MANY), BF16),
            jax.ShapeDtypeStruct((1, 2 * TOKENS), I32),
            jax.ShapeDtypeStruct((2 * TOKENS, 1), I32),
            jax.ShapeDtypeStruct((2 * TOKENS, 1), I32),
        ],
        compiler_params=pltpu.CompilerParams(vmem_limit_bytes=VMEM),
        cost_estimate=pl.CostEstimate(flops=256 * 1024 * width, bytes_accessed=7 << 20, transcendentals=0),
    )(flags, rows, *bottom, *bottom, wanted[None, :], wanted[:, None])


def table_kernel(probs, rows, b0, b1, b2, b3, few, go, by_row, lane_rank, row_rank, out, order, total, hits):
    vocab = out.shape[0]

    @pl.when(pl.program_id(0) == 0)
    def _():
        order[...] = jnp.zeros_like(order)
        hits[0] = jnp.max(lane_rank[...].astype(F32)).astype(I32) + 1

    def first():
        value = jnp.dot(probs[...], rows[...], preferred_element_type=F32)
        return value + jnp.dot(go[...], few[...], preferred_element_type=F32)

    out[...] = first().astype(BF16)

    @pl.when(hits[0] > MANY)
    def _():
        total[...] = first()

        @pl.loop(1, (hits[0] + MANY - 1) // MANY)
        def _(n):
            lie, there = lookup_picks(n * MANY, vocab, lane_rank[...], row_rank[...], by_row[...])
            more = lookup_sum(lie, rows, (b0, b1, b2, b3)).astype(BF16)
            total[...] += jnp.dot(there, more, preferred_element_type=F32)

        out[...] = total[...].astype(BF16)


def table_part(probs, rows, bottom, prepared):
    few, go, lane_rank, row_rank, wanted = prepared
    vocab, width = probs.shape[0], few.shape[1]
    step = 512
    return pl.pallas_call(
        table_kernel,
        grid=(width // step,),
        in_specs=[pl.BlockSpec((vocab, TOKENS), lambda n: (0, 0))]
        + [pl.BlockSpec((TOKENS, step), lambda n: (0, n))]
        + [pl.BlockSpec((8 * ROWS, step), lambda n: (0, n))] * 4
        + [
            pl.BlockSpec((MANY, step), lambda n: (0, n)),
            pl.BlockSpec((vocab, MANY), lambda n: (0, 0)),
            pl.BlockSpec((2 * TOKENS, 1), lambda n: (0, 0)),
            pl.BlockSpec((1, 2 * TOKENS), lambda n: (0, 0)),
            pl.BlockSpec((2 * TOKENS, 1), lambda n: (0, 0)),
        ],
        out_specs=[
            pl.BlockSpec((vocab, step), lambda n: (0, n)),
            pl.BlockSpec((8, 128), lambda n: (0, 0)),
        ],
        scratch_shapes=[pltpu.VMEM((vocab, step), F32), pltpu.SMEM((1,), I32)],
        out_shape=[jax.ShapeDtypeStruct((vocab, width), BF16), jax.ShapeDtypeStruct((8, 128), F32)],
        compiler_params=pltpu.CompilerParams(vmem_limit_bytes=VMEM),
        cost_estimate=pl.CostEstimate(flops=2 * 640 * vocab * width, bytes_accessed=20 << 20, transcendentals=0),
    )(probs, rows, *bottom, few, go, wanted, lane_rank, row_rank)


def digits_of(ids):
    digits = jnp.stack([ids // 256, ids % 256], axis=1)
    return jnp.pad(digits.astype(BF16), ((0, 0), (0, 126)))


def ids_of(codes):
    codes = codes.astype(I32)
    return codes[..., 0] * 256 + codes[..., 1]


def body(hidden, embedding, bottom_grad, targets, token_ids):
    width = hidden.shape[1]
    vocab = embedding.shape[0]
    section, tensor = lax.axis_index("section"), lax.axis_index("tensor")
    vocab_first = section * vocab
    z, yl, x, core = section // 8, (section // 4) % 2, section % 4, tensor % 2
    odd = (x + core) % 2
    x_place = (x - odd - core) // 2
    flags = jnp.stack([core, odd, yl, x_place % 2, z, vocab_first]).astype(I32)

    hidden = jnp.concatenate([hidden, digits_of(targets)], axis=1)
    bottom = jnp.concatenate([bottom_grad, digits_of(token_ids)], axis=1)
    chunks, lines = gather_rows(hidden, bottom)

    def wanted_of(pieces):
        ids = ids_of(jnp.stack([p[..., width : width + 2] for p in pieces]))
        ids = jnp.where(core == 0, ids, ids.transpose(1, 0, 2))
        return ids.reshape(2, 2, 4, ROWS).transpose(1, 0, 2, 3).reshape(CHUNK) - vocab_first

    wanted = [wanted_of(pieces) for pieces in chunks]


    kept, sent, rows = logits_part(flags, chunks, embedding)
    partial = kept + swap_core(sent)
    logits = partial + swap_half(partial.astype(F16)).astype(F32)
    picked = target_rows(flags, embedding, jnp.concatenate(wanted), partial)

    bottom = gather_rest(lines, partial[0, 0] > -1e30)
    prepared = lookup_rows(flags, rows, bottom, jnp.concatenate(wanted), vocab)

    stats = lax.all_to_all(stats_part(flags, logits, picked), "section", 0, 0, tiled=True)
    mine = probs_part(flags, stats, logits, bottom[1:])
    value, probs = input_part(flags, embedding, mine, swap_core(mine), picked)
    line = ring_sum(value, ring_b)

    table_grad, zeros = table_part(probs, rows, bottom, prepared)
    line = line + zeros[0, 0]
    pair = ring_sum(line.transpose(1, 0, 2, 3), ring_a)
    input_grad = pair[0] + swap_y(pair[1].astype(F16)).astype(F32)
    return ((input_grad * (1.0 / SCALE)).astype(BF16), table_grad)


def solution(mesh):
    split = P("section", "tensor")
    in_specs = (split, split, split, P("section"), P("section"))
    return jax.shard_map(body, mesh=mesh, in_specs=in_specs, out_specs=(split, split), check_vma=False)
```

time: 227 us -> 166 us (0.73)
  matrix products: 48.4 us -> 0 us
  Pallas kernels: 0 us -> 47.9 us
  local copies, waits for them, and re-layouts: 46 us -> 12 us
  waiting for transfers between devices: 76.1 us -> 46.6 us
  starting transfers between devices: 41.3 us -> 43.8 us
    dot_general x5 -> x0, matrix products: 48.4 us -> none  [the longest x1 16.1 us: body(): lax.dot_general(id_hits, lookup_rows, contract, preferred_element_type=F32)]
    pallas_call x0 -> x7, Pallas kernels: none -> 47.9 us  [the longest x1 13.1 us: logits_part(): pl.pallas_call(logits_kernel, grid_spec=pltpu.PrefetchScalarGridSpec(num_...]
    ppermute x24, waiting for transfers between devices: 67.6 us -> 38.2 us  [permute(): return lax.ppermute(value, BOTH, pairs)]
    gather x1 -> x0, local copies, waits for them, and re-layouts: 12.1 us -> none  [body(): jnp.take(embedding, jnp.clip(wanted, 0, vocab_rows - 1), axis=0).astype(F32)]
    dynamic_update_slice x18 -> x0, local copies, waits for them, and re-layouts: 11.1 us -> none  [put(): lax.dynamic_update_slice_in_dim(buffer, jnp.expand_dims(block, dim), inde...]
    unnamed x21 -> x13, local copies, waits for them, and re-layouts: 1.94 us -> 7.62 us
    transpose x2 -> x0, local copies, waits for them, and re-layouts: 5 us -> none  [the longest x1 2.81 us: body(): swap_core(sent).reshape(4, 4, rows, vocab_rows).transpose(1, 0, 2, 3)]
    ppermute x2 -> x0, local copies, waits for them, and re-layouts: 4.83 us -> none  [permute(): return lax.ppermute(value, BOTH, pairs)]
  transfers between devices with their start and end apart: 25 -> 25, of which waited for: 10 -> 14; matrix products, arithmetic and copies ran while one was open for 36% -> 6% of each run, Pallas kernels for 0% -> 23%
where the time goes in v2:
time: 166 us; the launch traced here: 165 us
  Pallas kernels  47.9 us (29%)
  waiting for transfers between devices  46.6 us (28%)
  starting transfers between devices  43.8 us (26%)
  other arithmetic  12.3 us (7%)
  local copies, waits for them, and re-layouts  12 us (7%)
  between operations  2.25 us (1%)
    ppermute x24, waiting for transfers between devices, permute(): return lax.ppermute(value, BOTH, pairs)  38.2 us
    ppermute x24, starting transfers between devices, permute(): return lax.ppermute(value, BOTH, pairs)  34.4 us
    pallas_call x1, Pallas kernels, logits_part(): pl.pallas_call(logits_kernel, grid_spec=pltpu.PrefetchScalarGridSpec(num_...  13.1 us
    pallas_call x1, Pallas kernels, table_part(): pl.pallas_call(table_kernel, grid=(width // step,), in_specs=[pl.BlockSpe...  11.9 us
    all_to_all x1, starting transfers between devices, body(): lax.all_to_all(stats_part(flags, logits, picked), 'section', 0, 0, tiled=...  9.45 us
    pallas_call x1, Pallas kernels, input_part(): pl.pallas_call(input_kernel, grid_spec=pltpu.PrefetchScalarGridSpec(num_s...  9.04 us
    all_to_all x1, waiting for transfers between devices, body(): lax.all_to_all(stats_part(flags, logits, picked), 'section', 0, 0, tiled=...  8.47 us
    unnamed x13, local copies, waits for them, and re-layouts  7.62 us
  transfers between devices with their start and end apart: 25, of which 14 were waited for; matrix products, arithmetic and copies ran while one was open for 6% of the time, Pallas kernels for 23%

profile of v2, /device:TPU:0, one launch (start us, length us, event | category | flops | bytes accessed | tf_op | source)
XLA Modules:
  0.0 164.9 jit_solution(14909335075066975641)
XLA Ops:
  2.2 0.9 fusion.13
  3.1 0.9 fusion.15
  4.0 4.0 %collective-permute-start.1 = (bf16[2,16,3200]{2,1,0:T(8,128)(2,1)S(1)}, bf16[2,16,3200]{2,1,0:T(8,128)(2,1)S(1)}, u32[]{:S(2)}, u32[]{:S(2)}) collective-permute-start(bf16[2,16,3200]{2,1,0:T(8,128)(2,1)S(1)} %get-tuple-element.37), channel_id=1, source_target_pairs={{0,64},{1,9},{2,66},{3,11},{4,68},{5,13},{6,70},{7,15},{8,72},{9,1... | collective-permute-start | bytes 614408 | tf_op jit(solution)/shard_map/ppermute | solution.py:35
  8.1 1.0 collective-permute-start
  9.1 2.2 %collective-permute-start.2 = (bf16[2,16,3200]{2,1,0:T(8,128)(2,1)S(1)}, bf16[2,16,3200]{2,1,0:T(8,128)(2,1)S(1)}, u32[]{:S(2)}, u32[]{:S(2)}) collective-permute-start(bf16[2,16,3200]{2,1,0:T(8,128)(2,1)S(1)} %get-tuple-element.37), channel_id=1, source_target_pairs={{0,96},{1,13},{2,98},{3,15},{4,100},{5,1},{6,102},{7,3},{8,104},{9... | collective-permute-start | bytes 614408 | tf_op jit(solution)/shard_map/ppermute | solution.py:35
  11.8 3.2 %collective-permute-done = bf16[2,16,3200]{2,1,0:T(8,128)(2,1)S(1)} collective-permute-done((bf16[2,16,3200]{2,1,0:T(8,128)(2,1)S(1)}, bf16[2,16,3200]{2,1,0:T(8,128)(2,1)S(1)}, u32[]{:S(2)}, u32[]{:S(2)}) %collective-permute-start) | collective-permute-done | bytes 204832 | tf_op jit(solution)/shard_map/ppermute | solution.py:35
  15.2 0.8 slice_bitcast_fusion.4
  16.0 1.6 collective-permute-start.4
  17.6 2.8 %collective-permute-start.6 = (bf16[4,16,3200]{2,1,0:T(8,128)(2,1)S(1)}, bf16[4,16,3200]{2,1,0:T(8,128)(2,1)S(1)}, u32[]{:S(2)}, u32[]{:S(2)}) collective-permute-start(bf16[4,16,3200]{2,1,0:T(8,128)(2,1)S(1)} %get-tuple-element.32.refs_0_), channel_id=1, source_target_pairs={{0,12},{1,97},{2,14},{3,99},{4,0},{5,101},{6,2},{7,103},{8,4},{9,1... | collective-permute-start | bytes 1228808 | tf_op jit(solution)/shard_map/ppermute | solution.py:35
  20.3 4.6 %collective-permute-done.4.refs_4_ = bf16[4,16,3200]{2,1,0:T(8,128)(2,1)S(1)} collective-permute-done((bf16[4,16,3200]{2,1,0:T(8,128)(2,1)S(1)}, bf16[4,16,3200]{2,1,0:T(8,128)(2,1)S(1)}, u32[]{:S(2)}, u32[]{:S(2)}) %collective-permute-start.4) | collective-permute-done | bytes 409632 | tf_op jit(solution)/shard_map/ppermute | solution.py:35
  26.9 2.2 %collective-permute-start.5 = (bf16[4,16,3200]{2,1,0:T(8,128)(2,1)}, bf16[4,16,3200]{2,1,0:T(8,128)(2,1)S(1)}, u32[]{:S(2)}, u32[]{:S(2)}) collective-permute-start(bf16[4,16,3200]{2,1,0:T(8,128)(2,1)} %broadcast_select_fusion), channel_id=1, source_target_pairs={{0,8},{1,65},{2,10},{3,67},{4,12},{5,69},{6,14},{7,71},{8,0},{9,73... | collective-permute-start | bytes 1228808 | tf_op jit(solution)/shard_map/ppermute | solution.py:35
  29.1 1.8 %collective-permute-start.9 = (bf16[4,16,3200]{2,1,0:T(8,128)(2,1)S(1)}, bf16[4,16,3200]{2,1,0:T(8,128)(2,1)S(1)}, u32[]{:S(2)}, u32[]{:S(2)}) collective-permute-start(bf16[4,16,3200]{2,1,0:T(8,128)(2,1)S(1)} %collective-permute-done.4.refs_4_), channel_id=1, source_target_pairs={{0,12},{1,97},{2,14},{3,99},{4,0},{5,101},{6,2},{7,103},{8,4},{9,1... | collective-permute-start | bytes 1228808 | tf_op jit(solution)/shard_map/ppermute | solution.py:35
  31.2 2.2 %collective-permute-start.8 = (bf16[4,16,3200]{2,1,0:T(8,128)(2,1)S(1)}, bf16[4,16,3200]{2,1,0:T(8,128)(2,1)S(1)}, u32[]{:S(2)}, u32[]{:S(2)}) collective-permute-start(bf16[4,16,3200]{2,1,0:T(8,128)(2,1)S(1)} %collective-permute-done.4.refs_4_), channel_id=1, source_target_pairs={{0,8},{1,65},{2,10},{3,67},{4,12},{5,69},{6,14},{7,71},{8,0},{9,73... | collective-permute-start | bytes 1228808 | tf_op jit(solution)/shard_map/ppermute | solution.py:35
  33.5 1.6 collective-permute-start.12
  35.3 1.3 collective-permute-done.5.refs_2_
  36.7 4.9 %collective-permute-done.9.refs_7_ = bf16[4,16,3200]{2,1,0:T(8,128)(2,1)S(1)} collective-permute-done((bf16[4,16,3200]{2,1,0:T(8,128)(2,1)S(1)}, bf16[4,16,3200]{2,1,0:T(8,128)(2,1)S(1)}, u32[]{:S(2)}, u32[]{:S(2)}) %collective-permute-start.9) | collective-permute-done | bytes 409632 | tf_op jit(solution)/shard_map/ppermute | solution.py:35
  41.7 3.6 %collective-permute-done.7.refs_5_ = bf16[4,16,3200]{2,1,0:T(8,128)(2,1)S(1)} collective-permute-done((bf16[4,16,3200]{2,1,0:T(8,128)(2,1)S(1)}, bf16[4,16,3200]{2,1,0:T(8,128)(2,1)S(1)}, u32[]{:S(2)}, u32[]{:S(2)}) %collective-permute-start.7) | collective-permute-done | bytes 409632 | tf_op jit(solution)/shard_map/ppermute | solution.py:35
  45.3 13.1 %shard_map.68 = (f32[1600,256]{1,0:T(8,128)}, f32[1600,256]{1,0:T(8,128)}, bf16[512,3072]{1,0:T(8,128)(2,1)}) custom-call(s32[6]{0:T(128)S(1)} %stack.105.flags, bf16[4,16,3200]{2,1,0:T(8,128)(2,1)S(1)} %get-tuple-element.32.refs_0_, bf16[4,16,3200]{2,1,0:T(8,128)(2,1)S(1)} %collective-permute-done.3.refs_1_, ...), custom_call_target="tpu_custom_call" | custom-call | flops 5033164800 | bytes 16777216 | tf_op jit(solution)/shard_map/pallas_call | solution.py:145
  59.2 3.2 %collective-permute-done.10 = f32[1600,256]{1,0:T(8,128)} collective-permute-done((f32[1600,256]{1,0:T(8,128)}, f32[1600,256]{1,0:T(8,128)}, u32[]{:S(2)}, u32[]{:S(2)}) %collective-permute-start.10) | collective-permute-done | bytes 1638432 | tf_op jit(solution)/shard_map/ppermute | solution.py:35
  62.4 2.3 %fusion.26 = (f16[1600,256]{1,0:T(8,128)(2,1)S(1)}, f32[1600,256]{1,0:T(8,128)S(1)}) fusion(f32[1600,256]{1,0:T(8,128)} %get-tuple-element.14, f32[1600,256]{1,0:T(8,128)} %collective-permute-done.10), kind=kLoop, calls=%fused_computation.76 | loop fusion | flops 819200 | bytes 5734400 | tf_op jit(solution)/shard_map/convert_element_type | solution.py:526
  64.7 3.3 %collective-permute-start.11 = (f16[1600,256]{1,0:T(8,128)(2,1)S(1)}, f16[1600,256]{1,0:T(8,128)(2,1)}, u32[]{:S(2)}, u32[]{:S(2)}) collective-permute-start(f16[1600,256]{1,0:T(8,128)(2,1)S(1)} %get-tuple-element.26), channel_id=1, source_target_pairs={{0,2},{1,3},{2,0},{3,1},{4,6},{5,7},{6,4},{7,5},{8,10},{9,11},{10,... | collective-permute-start | bytes 2457608 | tf_op jit(solution)/shard_map/ppermute | solution.py:35
  69.3 2.0 %maximum_select_fusion = bf16[8,16,3200]{2,1,0:T(8,128)(2,1)} fusion(bf16[4,16,3200]{2,1,0:T(8,128)(2,1)} %collective-permute-done.12, bf16[4,16,3200]{2,1,0:T(8,128)(2,1)S(1)} %copy-done.5, pred[]{:T(512)} %bitcast.39), kind=kLoop, calls=%fused_computation.7 | loop fusion | flops 819200 | bytes 1638401 | tf_op jit(solution)/shard_map/jit(_where)/select_n | solution.py:76
  71.3 3.3 %collective-permute-start.15 = (bf16[8,16,3200]{2,1,0:T(8,128)(2,1)}, bf16[8,16,3200]{2,1,0:T(8,128)(2,1)}, u32[]{:S(2)}, u32[]{:S(2)}) collective-permute-start(bf16[8,16,3200]{2,1,0:T(8,128)(2,1)} %maximum_select_fusion), channel_id=1, source_target_pairs={{0,12},{1,97},{2,14},{3,99},{4,0},{5,101},{6,2},{7,103},{8,4},{9,1... | collective-permute-start | bytes 2457608 | tf_op jit(solution)/shard_map/ppermute | solution.py:35
  75.5 3.8 %copy-done.2 = bf16[1600,3072]{1,0:T(8,128)(2,1)S(1)} copy-done((bf16[1600,3072]{1,0:T(8,128)(2,1)S(1)}, bf16[1600,3072]{1,0:T(8,128)(2,1)}, u32[]{:S(2)}) %copy-start.2) | copy-done | bytes 9830424
  79.3 5.4 %shard_map.69.after.picked = bf16[4,2,4,16,3072]{4,3,2,1,0:T(8,128)(2,1)S(1)} custom-call(s32[6]{0:T(128)S(1)} %stack.105.flags, bf16[1600,3072]{1,0:T(8,128)(2,1)S(1)} %copy-done.2, s32[1,512]{1,0:T(1,128)S(1)} %bitcast.118, s32[512,1]{1,0:T(8,128)S(1)} %copy.86.by_row.far, f32[1600,256]{1,0:T(8,128)S(1)} %get-tuple-element.27.after), custom_call_target="tpu_custom_call" | custom-call | flops 2516582400 | bytes 14680064 | tf_op jit(solution)/shard_map/pallas_call | solution.py:296
  84.7 1.9 %collective-permute-done.11 = f16[1600,256]{1,0:T(8,128)(2,1)} collective-permute-done((f16[1600,256]{1,0:T(8,128)(2,1)S(1)}, f16[1600,256]{1,0:T(8,128)(2,1)}, u32[]{:S(2)}, u32[]{:S(2)}) %collective-permute-start.11) | collective-permute-done | bytes 819232 | tf_op jit(solution)/shard_map/ppermute | solution.py:35
  86.6 1.3 convert_add_fusion.logits
  88.0 1.9 %shard_map.70 = f32[32,2,256]{2,1,0:T(2,128)} custom-call(s32[6]{0:T(128)S(1)} %stack.105.flags, f32[1600,256]{1,0:T(8,128)S(1)} %convert_add_fusion.logits, bf16[4,2,4,16,3072]{4,3,2,1,0:T(8,128)(2,1)S(1)} %shard_map.69.after.picked), custom_call_target="tpu_custom_call" | custom-call | flops 1048576 | bytes 2097152 | tf_op jit(solution)/shard_map/pallas_call | solution.py:191
  89.8 9.4 %all-to-all-start = ((f32[32,2,256]{2,1,0:T(2,128)}), f32[32,2,256]{2,1,0:T(2,128)S(1)}, u32[]{:S(2)}, u32[]{:S(2)}) async-start(f32[32,2,256]{2,1,0:T(2,128)} %shard_map.70), calls=%async_computation | async-start | bytes 131072 | tf_op jit(solution)/shard_map/all_to_all | solution.py:532
  99.3 8.5 %all-to-all-done.stats = f32[32,2,256]{2,1,0:T(2,128)S(1)} async-done(((f32[32,2,256]{2,1,0:T(2,128)}), f32[32,2,256]{2,1,0:T(2,128)S(1)}, u32[]{:S(2)}, u32[]{:S(2)}) %all-to-all-start) | async-done | bytes 65568 | tf_op jit(solution)/shard_map/all_to_all | solution.py:532
  107.8 1.2 shard_map.71.kept
  109.1 2.3 %collective-permute-done.16.got = bf16[1600,256]{1,0:T(8,128)(2,1)S(1)} collective-permute-done((bf16[1600,256]{1,0:T(8,128)(2,1)S(1)}, bf16[1600,256]{1,0:T(8,128)(2,1)S(1)}, u32[]{:S(2)}, u32[]{:S(2)}) %collective-permute-start.16) | collective-permute-done | bytes 819232 | tf_op jit(solution)/shard_map/ppermute | solution.py:35
  111.4 3.8 %copy-done.3 = bf16[1600,3072]{1,0:T(8,128)(2,1)S(1)} copy-done((bf16[1600,3072]{1,0:T(8,128)(2,1)S(1)}, bf16[1600,3072]{1,0:T(8,128)(2,1)}, u32[]{:S(2)}) %copy-start.3) | copy-done | bytes 9830424
  115.2 9.0 %shard_map.72 = (f32[4,2,4,16,3072]{4,3,2,1,0:T(8,128)S(1)}, bf16[1600,512]{1,0:T(8,128)(2,1)S(1)}) custom-call(s32[6]{0:T(128)S(1)} %stack.105.flags, bf16[1600,256]{1,0:T(8,128)(2,1)S(1)} %shard_map.71.kept, bf16[1600,256]{1,0:T(8,128)(2,1)S(1)} %collective-permute-done.16.got, bf16[1600,3072]{1,0:T(8,128)(2,1)S(1)} %copy-done.3, ...), custom_call_target="tpu_custom_call" | custom-call | flops 5033164800 | bytes 16777216 | tf_op jit(solution)/shard_map/pallas_call | solution.py:340
  125.2 1.1 collective-permute-start.17
  126.3 1.0 collective-permute-start.19
  127.3 1.0 collective-permute-start.18
  128.3 5.3 %shard_map.73 = (bf16[128,3072]{1,0:T(8,128)(2,1)S(1)}, bf16[1600,128]{1,0:T(8,128)(2,1)S(1)}, s32[1,1024]{1,0:T(1,128)S(1)}, s32[1024,1]{1,0:T(8,128)S(1)}, s32[1024,1]{1,0:T(8,128)S(1)}) custom-call(s32[6]{0:T(128)S(1)} %stack.105.flags, bf16[512,3072]{1,0:T(8,128)(2,1)S(1)} %copy-done.4, bf16[128,3200]{1,0:T(8,128)(2,1)} %bitcast.48.b0.c0, ...), custom_call_target="tpu_custom_call" | custom-call | flops 805306368 | bytes 7340032 | tf_op jit(solution)/shard_map/pallas_call | solution.py:407
  133.6 11.9 %shard_map.74 = (bf16[1600,3072]{1,0:T(8,128)(2,1)}, f32[8,128]{1,0:T(8,128)S(1)}) custom-call(bf16[1600,512]{1,0:T(8,128)(2,1)S(1)} %get-tuple-element.17.probs, bf16[512,3072]{1,0:T(8,128)(2,1)S(1)} %copy-done.4, bf16[128,3200]{1,0:T(8,128)(2,1)} %bitcast.48.b0.c0, bf16[128,3200]{1,0:T(8,128)(2,1)} %bitcast.41.after0.b1.c1, ...), custom_call_target="tpu_custom_call" | custom-call | flops 6291456000 | bytes 20971520 | tf_op jit(solution)/shard_map/pallas_call | solution.py:468
  146.0 1.9 %collective-permute-done.19 = f16[2,4,16,3072]{3,2,1,0:T(8,128)(2,1)S(1)} collective-permute-done((f16[2,4,16,3072]{3,2,1,0:T(8,128)(2,1)S(1)}, f16[2,4,16,3072]{3,2,1,0:T(8,128)(2,1)S(1)}, u32[]{:S(2)}, u32[]{:S(2)}) %collective-permute-start.19) | collective-permute-done | bytes 786464 | tf_op jit(solution)/shard_map/ppermute | solution.py:35
  147.9 1.2 fusion.4
  149.3 1.2 collective-permute-start.20
  150.5 0.9 collective-permute-start.22
  151.4 1.3 collective-permute-start.21
  152.6 2.4 %collective-permute-done.20 = f16[2,16,3072]{2,1,0:T(8,128)(2,1)S(1)} collective-permute-done((f16[2,16,3072]{2,1,0:T(8,128)(2,1)S(1)}, f16[2,16,3072]{2,1,0:T(8,128)(2,1)S(1)}, u32[]{:S(2)}, u32[]{:S(2)}) %collective-permute-start.20) | collective-permute-done | bytes 196640 | tf_op jit(solution)/shard_map/ppermute | solution.py:35
  155.0 4.5 %collective-permute-done.22 = f16[2,16,3072]{2,1,0:T(8,128)(2,1)S(1)} collective-permute-done((f16[2,16,3072]{2,1,0:T(8,128)(2,1)S(1)}, f16[2,16,3072]{2,1,0:T(8,128)(2,1)S(1)}, u32[]{:S(2)}, u32[]{:S(2)}) %collective-permute-start.22) | collective-permute-done | bytes 196640 | tf_op jit(solution)/shard_map/ppermute | solution.py:35
  159.6 0.8 collective-permute-start.23
  160.4 3.8 %collective-permute-done.23 = f16[16,3072]{1,0:T(8,128)(2,1)S(1)} collective-permute-done((f16[16,3072]{1,0:T(8,128)(2,1)S(1)}, f16[16,3072]{1,0:T(8,128)(2,1)S(1)}, u32[]{:S(2)}, u32[]{:S(2)}) %collective-permute-start.23) | collective-permute-done | bytes 98336 | tf_op jit(solution)/shard_map/ppermute | solution.py:35
  (78 shorter events, 8.9 us)
Async XLA Ops:
  4.0 7.8 %collective-permute-start.1 = (bf16[2,16,3200]{2,1,0:T(8,128)(2,1)S(1)}, bf16[2,16,3200]{2,1,0:T(8,128)(2,1)S(1)}, u32[]{:S(2)}, u32[]{:S(2)}) collective-permute-start(bf16[2,16,3200]{2,1,0:T(8,128)(2,1)S(1)} %get-tuple-element.37), channel_id=1, source_target_pairs={{0,64},{1,9},{2,66},{3,11},{4,68},{5,13},{6,70},{7,15},{8,72},{9,1... | collective-permute-start | bytes 614408 | tf_op jit(solution)/shard_map/ppermute | solution.py:35
  8.1 7.0 %collective-permute-start = (bf16[2,16,3200]{2,1,0:T(8,128)(2,1)S(1)}, bf16[2,16,3200]{2,1,0:T(8,128)(2,1)S(1)}, u32[]{:S(2)}, u32[]{:S(2)}) collective-permute-start(bf16[2,16,3200]{2,1,0:T(8,128)(2,1)S(1)} %get-tuple-element.37), channel_id=1, source_target_pairs={{0,32},{1,5},{2,34},{3,7},{4,36},{5,9},{6,38},{7,11},{8,40},{9,13}... | collective-permute-start | bytes 614408 | tf_op jit(solution)/shard_map/ppermute | solution.py:35
  9.1 6.0 %collective-permute-start.2 = (bf16[2,16,3200]{2,1,0:T(8,128)(2,1)S(1)}, bf16[2,16,3200]{2,1,0:T(8,128)(2,1)S(1)}, u32[]{:S(2)}, u32[]{:S(2)}) collective-permute-start(bf16[2,16,3200]{2,1,0:T(8,128)(2,1)S(1)} %get-tuple-element.37), channel_id=1, source_target_pairs={{0,96},{1,13},{2,98},{3,15},{4,100},{5,1},{6,102},{7,3},{8,104},{9... | collective-permute-start | bytes 614408 | tf_op jit(solution)/shard_map/ppermute | solution.py:35
  16.0 8.9 %collective-permute-start.4 = (bf16[4,16,3200]{2,1,0:T(8,128)(2,1)S(1)}, bf16[4,16,3200]{2,1,0:T(8,128)(2,1)S(1)}, u32[]{:S(2)}, u32[]{:S(2)}) collective-permute-start(bf16[4,16,3200]{2,1,0:T(8,128)(2,1)S(1)} %get-tuple-element.32.refs_0_), channel_id=1, source_target_pairs={{0,16},{1,17},{2,18},{3,19},{4,20},{5,21},{6,22},{7,23},{8,24},{9,... | collective-permute-start | bytes 1228808 | tf_op jit(solution)/shard_map/ppermute | solution.py:35
  17.6 13.5 %collective-permute-start.6 = (bf16[4,16,3200]{2,1,0:T(8,128)(2,1)S(1)}, bf16[4,16,3200]{2,1,0:T(8,128)(2,1)S(1)}, u32[]{:S(2)}, u32[]{:S(2)}) collective-permute-start(bf16[4,16,3200]{2,1,0:T(8,128)(2,1)S(1)} %get-tuple-element.32.refs_0_), channel_id=1, source_target_pairs={{0,12},{1,97},{2,14},{3,99},{4,0},{5,101},{6,2},{7,103},{8,4},{9,1... | collective-permute-start | bytes 1228808 | tf_op jit(solution)/shard_map/ppermute | solution.py:35
  20.3 13.2 %collective-permute-start.3 = (bf16[4,16,3200]{2,1,0:T(8,128)(2,1)S(1)}, bf16[4,16,3200]{2,1,0:T(8,128)(2,1)S(1)}, u32[]{:S(2)}, u32[]{:S(2)}) collective-permute-start(bf16[4,16,3200]{2,1,0:T(8,128)(2,1)S(1)} %get-tuple-element.32.refs_0_), channel_id=1, source_target_pairs={{0,4},{1,33},{2,6},{3,35},{4,8},{5,37},{6,10},{7,39},{8,12},{9,41}... | collective-permute-start | bytes 1228808 | tf_op jit(solution)/shard_map/ppermute | solution.py:35
  26.9 9.7 %collective-permute-start.5 = (bf16[4,16,3200]{2,1,0:T(8,128)(2,1)}, bf16[4,16,3200]{2,1,0:T(8,128)(2,1)S(1)}, u32[]{:S(2)}, u32[]{:S(2)}) collective-permute-start(bf16[4,16,3200]{2,1,0:T(8,128)(2,1)} %broadcast_select_fusion), channel_id=1, source_target_pairs={{0,8},{1,65},{2,10},{3,67},{4,12},{5,69},{6,14},{7,71},{8,0},{9,73... | collective-permute-start | bytes 1228808 | tf_op jit(solution)/shard_map/ppermute | solution.py:35
  29.1 12.5 %collective-permute-start.9 = (bf16[4,16,3200]{2,1,0:T(8,128)(2,1)S(1)}, bf16[4,16,3200]{2,1,0:T(8,128)(2,1)S(1)}, u32[]{:S(2)}, u32[]{:S(2)}) collective-permute-start(bf16[4,16,3200]{2,1,0:T(8,128)(2,1)S(1)} %collective-permute-done.4.refs_4_), channel_id=1, source_target_pairs={{0,12},{1,97},{2,14},{3,99},{4,0},{5,101},{6,2},{7,103},{8,4},{9,1... | collective-permute-start | bytes 1228808 | tf_op jit(solution)/shard_map/ppermute | solution.py:35
  31.2 10.5 %collective-permute-start.8 = (bf16[4,16,3200]{2,1,0:T(8,128)(2,1)S(1)}, bf16[4,16,3200]{2,1,0:T(8,128)(2,1)S(1)}, u32[]{:S(2)}, u32[]{:S(2)}) collective-permute-start(bf16[4,16,3200]{2,1,0:T(8,128)(2,1)S(1)} %collective-permute-done.4.refs_4_), channel_id=1, source_target_pairs={{0,8},{1,65},{2,10},{3,67},{4,12},{5,69},{6,14},{7,71},{8,0},{9,73... | collective-permute-start | bytes 1228808 | tf_op jit(solution)/shard_map/ppermute | solution.py:35
  33.4 11.9 %collective-permute-start.7 = (bf16[4,16,3200]{2,1,0:T(8,128)(2,1)S(1)}, bf16[4,16,3200]{2,1,0:T(8,128)(2,1)S(1)}, u32[]{:S(2)}, u32[]{:S(2)}) collective-permute-start(bf16[4,16,3200]{2,1,0:T(8,128)(2,1)S(1)} %collective-permute-done.4.refs_4_), channel_id=1, source_target_pairs={{0,4},{1,33},{2,6},{3,35},{4,8},{5,37},{6,10},{7,39},{8,12},{9,41}... | collective-permute-start | bytes 1228808 | tf_op jit(solution)/shard_map/ppermute | solution.py:35
  33.5 35.8 %collective-permute-start.12 = (bf16[4,16,3200]{2,1,0:T(8,128)(2,1)}, bf16[4,16,3200]{2,1,0:T(8,128)(2,1)}, u32[]{:S(2)}, u32[]{:S(2)}) collective-permute-start(bf16[4,16,3200]{2,1,0:T(8,128)(2,1)} %get-tuple-element.31), channel_id=1, source_target_pairs={{0,16},{1,17},{2,18},{3,19},{4,20},{5,21},{6,22},{7,23},{8,24},{9,... | collective-permute-start | bytes 1228808 | tf_op jit(solution)/shard_map/ppermute | solution.py:35
  58.5 3.9 %collective-permute-start.10 = (f32[1600,256]{1,0:T(8,128)}, f32[1600,256]{1,0:T(8,128)}, u32[]{:S(2)}, u32[]{:S(2)}) collective-permute-start(f32[1600,256]{1,0:T(8,128)} %get-tuple-element.15), channel_id=1, source_target_pairs={{0,1},{1,0},{2,3},{3,2},{4,5},{5,4},{6,7},{7,6},{8,9},{9,8},{10,11... | collective-permute-start | bytes 4915208 | tf_op jit(solution)/shard_map/ppermute | solution.py:35
  62.4 6.9 %copy-start.5 = (bf16[4,16,3200]{2,1,0:T(8,128)(2,1)S(1)}, bf16[4,16,3200]{2,1,0:T(8,128)(2,1)}, u32[]{:S(2)}) copy-start(bf16[4,16,3200]{2,1,0:T(8,128)(2,1)} %get-tuple-element.31) | copy-start | bytes 1228804
  64.7 22.0 %collective-permute-start.11 = (f16[1600,256]{1,0:T(8,128)(2,1)S(1)}, f16[1600,256]{1,0:T(8,128)(2,1)}, u32[]{:S(2)}, u32[]{:S(2)}) collective-permute-start(f16[1600,256]{1,0:T(8,128)(2,1)S(1)} %get-tuple-element.26), channel_id=1, source_target_pairs={{0,2},{1,3},{2,0},{3,1},{4,6},{5,7},{6,4},{7,5},{8,10},{9,11},{10,... | collective-permute-start | bytes 2457608 | tf_op jit(solution)/shard_map/ppermute | solution.py:35
  71.3 28.0 %collective-permute-start.15 = (bf16[8,16,3200]{2,1,0:T(8,128)(2,1)}, bf16[8,16,3200]{2,1,0:T(8,128)(2,1)}, u32[]{:S(2)}, u32[]{:S(2)}) collective-permute-start(bf16[8,16,3200]{2,1,0:T(8,128)(2,1)} %maximum_select_fusion), channel_id=1, source_target_pairs={{0,12},{1,97},{2,14},{3,99},{4,0},{5,101},{6,2},{7,103},{8,4},{9,1... | collective-permute-start | bytes 2457608 | tf_op jit(solution)/shard_map/ppermute | solution.py:35
  74.6 24.7 %collective-permute-start.14 = (bf16[8,16,3200]{2,1,0:T(8,128)(2,1)}, bf16[8,16,3200]{2,1,0:T(8,128)(2,1)}, u32[]{:S(2)}, u32[]{:S(2)}) collective-permute-start(bf16[8,16,3200]{2,1,0:T(8,128)(2,1)} %maximum_select_fusion), channel_id=1, source_target_pairs={{0,8},{1,65},{2,10},{3,67},{4,12},{5,69},{6,14},{7,71},{8,0},{9,73... | collective-permute-start | bytes 2457608 | tf_op jit(solution)/shard_map/ppermute | solution.py:35
  74.7 24.6 %collective-permute-start.13 = (bf16[8,16,3200]{2,1,0:T(8,128)(2,1)}, bf16[8,16,3200]{2,1,0:T(8,128)(2,1)}, u32[]{:S(2)}, u32[]{:S(2)}) collective-permute-start(bf16[8,16,3200]{2,1,0:T(8,128)(2,1)} %maximum_select_fusion), channel_id=1, source_target_pairs={{0,4},{1,33},{2,6},{3,35},{4,8},{5,37},{6,10},{7,39},{8,12},{9,41}... | collective-permute-start | bytes 2457608 | tf_op jit(solution)/shard_map/ppermute | solution.py:35
  75.5 3.8 %copy-start.2 = (bf16[1600,3072]{1,0:T(8,128)(2,1)S(1)}, bf16[1600,3072]{1,0:T(8,128)(2,1)}, u32[]{:S(2)}) copy-start(bf16[1600,3072]{1,0:T(8,128)(2,1)} %table.3) | copy-start | bytes 29491204
  84.7 3.3 %copy-start = (bf16[4,2,4,16,3072]{4,3,2,1,0:T(8,128)(2,1)}, bf16[4,2,4,16,3072]{4,3,2,1,0:T(8,128)(2,1)S(1)}, u32[]{:S(2)}) copy-start(bf16[4,2,4,16,3072]{4,3,2,1,0:T(8,128)(2,1)S(1)} %shard_map.69.after.picked) | copy-start | bytes 9437188
  89.8 18.0 %all-to-all-start = ((f32[32,2,256]{2,1,0:T(2,128)}), f32[32,2,256]{2,1,0:T(2,128)S(1)}, u32[]{:S(2)}, u32[]{:S(2)}) async-start(f32[32,2,256]{2,1,0:T(2,128)} %shard_map.70), calls=%async_computation | async-start | bytes 131072 | tf_op jit(solution)/shard_map/all_to_all | solution.py:532
  107.8 3.6 %copy-start.1 = (bf16[4,2,4,16,3072]{4,3,2,1,0:T(8,128)(2,1)S(1)}, bf16[4,2,4,16,3072]{4,3,2,1,0:T(8,128)(2,1)}, u32[]{:S(2)}) copy-start(bf16[4,2,4,16,3072]{4,3,2,1,0:T(8,128)(2,1)} %copy-done) | copy-start | bytes 9437188
  109.0 2.4 %collective-permute-start.16 = (bf16[1600,256]{1,0:T(8,128)(2,1)S(1)}, bf16[1600,256]{1,0:T(8,128)(2,1)S(1)}, u32[]{:S(2)}, u32[]{:S(2)}) collective-permute-start(bf16[1600,256]{1,0:T(8,128)(2,1)S(1)} %shard_map.71.kept), channel_id=1, source_target_pairs={{0,1},{1,0},{2,3},{3,2},{4,5},{5,4},{6,7},{7,6},{8,9},{9,8},{10,11... | collective-permute-start | bytes 2457608 | tf_op jit(solution)/shard_map/ppermute | solution.py:35
  111.4 3.8 %copy-start.3 = (bf16[1600,3072]{1,0:T(8,128)(2,1)S(1)}, bf16[1600,3072]{1,0:T(8,128)(2,1)}, u32[]{:S(2)}) copy-start(bf16[1600,3072]{1,0:T(8,128)(2,1)} %table.3) | copy-start | bytes 29491204
  124.8 3.6 %copy-start.4 = (bf16[512,3072]{1,0:T(8,128)(2,1)S(1)}, bf16[512,3072]{1,0:T(8,128)(2,1)}, u32[]{:S(2)}) copy-start(bf16[512,3072]{1,0:T(8,128)(2,1)} %get-tuple-element.18.rows) | copy-start | bytes 9437188
  125.2 20.8 %collective-permute-start.17 = (f16[2,4,16,3072]{3,2,1,0:T(8,128)(2,1)S(1)}, f16[2,4,16,3072]{3,2,1,0:T(8,128)(2,1)S(1)}, u32[]{:S(2)}, u32[]{:S(2)}) collective-permute-start(f16[2,4,16,3072]{3,2,1,0:T(8,128)(2,1)S(1)} %get-tuple-element.28), channel_id=1, source_target_pairs={{0,12},{1,97},{2,14},{3,99},{4,0},{5,101},{6,2},{7,103},{8,4},{9,1... | collective-permute-start | bytes 2359304 | tf_op jit(solution)/shard_map/ppermute | solution.py:35
  126.3 21.6 %collective-permute-start.19 = (f16[2,4,16,3072]{3,2,1,0:T(8,128)(2,1)S(1)}, f16[2,4,16,3072]{3,2,1,0:T(8,128)(2,1)S(1)}, u32[]{:S(2)}, u32[]{:S(2)}) collective-permute-start(f16[2,4,16,3072]{3,2,1,0:T(8,128)(2,1)S(1)} %get-tuple-element.29), channel_id=1, source_target_pairs={{0,4},{1,33},{2,6},{3,35},{4,8},{5,37},{6,10},{7,39},{8,12},{9,41}... | collective-permute-start | bytes 2359304 | tf_op jit(solution)/shard_map/ppermute | solution.py:35
  127.3 20.6 %collective-permute-start.18 = (f16[2,4,16,3072]{3,2,1,0:T(8,128)(2,1)S(1)}, f16[2,4,16,3072]{3,2,1,0:T(8,128)(2,1)S(1)}, u32[]{:S(2)}, u32[]{:S(2)}) collective-permute-start(f16[2,4,16,3072]{3,2,1,0:T(8,128)(2,1)S(1)} %get-tuple-element.30), channel_id=1, source_target_pairs={{0,8},{1,65},{2,10},{3,67},{4,12},{5,69},{6,14},{7,71},{8,0},{9,73... | collective-permute-start | bytes 2359304 | tf_op jit(solution)/shard_map/ppermute | solution.py:35
  149.3 5.7 %collective-permute-start.20 = (f16[2,16,3072]{2,1,0:T(8,128)(2,1)S(1)}, f16[2,16,3072]{2,1,0:T(8,128)(2,1)S(1)}, u32[]{:S(2)}, u32[]{:S(2)}) collective-permute-start(f16[2,16,3072]{2,1,0:T(8,128)(2,1)S(1)} %get-tuple-element.33), channel_id=1, source_target_pairs={{0,96},{1,13},{2,98},{3,15},{4,100},{5,1},{6,102},{7,3},{8,104},{9... | collective-permute-start | bytes 589832 | tf_op jit(solution)/shard_map/ppermute | solution.py:35
  150.5 9.0 %collective-permute-start.22 = (f16[2,16,3072]{2,1,0:T(8,128)(2,1)S(1)}, f16[2,16,3072]{2,1,0:T(8,128)(2,1)S(1)}, u32[]{:S(2)}, u32[]{:S(2)}) collective-permute-start(f16[2,16,3072]{2,1,0:T(8,128)(2,1)S(1)} %get-tuple-element.34), channel_id=1, source_target_pairs={{0,32},{1,5},{2,34},{3,7},{4,36},{5,9},{6,38},{7,11},{8,40},{9,13}... | collective-permute-start | bytes 589832 | tf_op jit(solution)/shard_map/ppermute | solution.py:35
  151.4 8.1 %collective-permute-start.21 = (f16[2,16,3072]{2,1,0:T(8,128)(2,1)S(1)}, f16[2,16,3072]{2,1,0:T(8,128)(2,1)S(1)}, u32[]{:S(2)}, u32[]{:S(2)}) collective-permute-start(f16[2,16,3072]{2,1,0:T(8,128)(2,1)S(1)} %get-tuple-element.35), channel_id=1, source_target_pairs={{0,64},{1,9},{2,66},{3,11},{4,68},{5,13},{6,70},{7,15},{8,72},{9,1... | collective-permute-start | bytes 589832 | tf_op jit(solution)/shard_map/ppermute | solution.py:35
  159.6 4.7 %collective-permute-start.23 = (f16[16,3072]{1,0:T(8,128)(2,1)S(1)}, f16[16,3072]{1,0:T(8,128)(2,1)S(1)}, u32[]{:S(2)}, u32[]{:S(2)}) collective-permute-start(f16[16,3072]{1,0:T(8,128)(2,1)S(1)} %fusion.16), channel_id=1, source_target_pairs={{0,16},{1,17},{2,18},{3,19},{4,20},{5,21},{6,22},{7,23},{8,24},{9,... | collective-permute-start | bytes 294920 | tf_op jit(solution)/shard_map/ppermute | solution.py:35
